TPU v7x, 256 devices: a whole 4x4x8 slice. The times are simulated.
256 devices in a mesh: orb: 16 (over x_lo, y, core), dom: 16 (over x_hi, z).
Axes of the slice: x: 4 (x_hi: 2, x_lo: 2; x = x_hi * 2 + x_lo), y: 4, z: 8, core: 2. Of those that a mesh axis runs over, the one named last changes fastest.
Arguments:
- orbitals: bfloat16 [128, 48, 4096], P('orb', 'dom'), may hold values from -6 to 6
- block_owner: int32 [1], replicated, may hold values from 0 to 15
Outputs:
- exchange_applied: bfloat16 [128, 48, 4096], P('orb', 'dom')
- intersection: float32 [128, 8], P('orb')
Inputs may be any that keep to these rules, and one draw needn't show every extreme that they name: `block_owner`: one block index for the round.
All inputs are finite; a program needn't handle non-finite values.
Results may differ from a plain program's by a relative error of at most 0.003.
Values may be sent and summed in bfloat16 or wider, within the bound.
No kernel may reach another device: no remote copies, remote signals or barrier semaphores. Data moves between devices by JAX's collectives and lax.ppermute only.
A program may use at most 128 MiB of HBM per device.

v0:
```python
import jax
import jax.numpy as jnp
from jax import lax
from jax.sharding import PartitionSpec as P

NY = 64
BLK = 8
SWEEPS = 4


inv_diag = 1.0 / 6.02


def broadcast(block, axis, owner):
    block = jnp.where(lax.axis_index(axis) == owner, block, jnp.zeros_like(block))
    return lax.psum(block, axis)


def with_halo(block, sides, width):
    for axis, dim in sides:
        count = lax.axis_size(axis)
        forward = [(i, i + 1) for i in range(count - 1)]
        forward.append((count - 1, 0))
        backward = [(target, source) for source, target in forward]
        low = lax.ppermute(
            lax.slice_in_dim(block, block.shape[dim] - width, None, axis=dim), axis, forward
        )
        high = lax.ppermute(lax.slice_in_dim(block, 0, width, axis=dim), axis, backward)
        block = jnp.concatenate([low, block, high], axis=dim)
    return block


def plane_sum(field):
    column = lax.broadcasted_iota(jnp.int32, (field.shape[-1],), 0) % NY
    lower = jnp.where(column == 0, jnp.roll(field, 1 - NY, -1), jnp.roll(field, 1, -1))
    upper = jnp.where(column == NY - 1, jnp.roll(field, NY - 1, -1), jnp.roll(field, -1, -1))
    return lower + upper + jnp.roll(field, NY, -1) + jnp.roll(field, -NY, -1)


def density(block_part, own_part):
    pairs = block_part.shape[0] * own_part.shape[0]
    product = block_part.astype(jnp.float32)[:, None] * own_part.astype(jnp.float32)[None, :]
    return product.reshape(pairs, own_part.shape[1], own_part.shape[2])


def on_device(orbitals, block_owner):
    own_count, depth, plane = orbitals.shape
    per_group = own_count // BLK
    index = block_owner[0]
    owner = index // per_group
    phi = broadcast(orbitals, "orb", owner)
    phif = phi.astype(jnp.float32)
    pot = density(phi, orbitals) * inv_diag
    for sweep in range(SWEEPS - 1):
        wide = with_halo(pot.astype(jnp.bfloat16), (("dom", 1),), 1).astype(pot.dtype)
        near = wide[:, 2:] + wide[:, :-2] + plane_sum(pot)
        pot = (density(phi, orbitals) + near) * inv_diag
    pot = pot.reshape(BLK, own_count, depth, plane)
    applied = (-jnp.sum(pot * phif[:, None], axis=0)).astype(jnp.bfloat16)
    flat_app = applied.reshape(own_count, depth * plane)
    flat_own = orbitals.reshape(own_count, depth * plane)
    partial_prod = lax.dot_general(
        flat_own, flat_app, (((1,), (1,)), ((), ())), preferred_element_type=jnp.float32
    )
    total = lax.psum(partial_prod, "dom") / 512.0
    return (applied, total)


def solution(mesh):
    in_specs = (P("orb", "dom", None), P())
    out_specs = (P("orb", "dom", None), P("orb", None))
    return jax.shard_map(
        on_device, mesh=mesh, in_specs=in_specs, out_specs=out_specs, check_vma=False
    )
```

profile of v0, /device:TPU:16, one launch (start us, length us, event | category | flops | bytes accessed | tf_op | source)
XLA Modules:
  0.0 275.0 jit_solution(9693216560261602966)
XLA Ops:
  7.9 1.7 broadcast_select_fusion
  9.7 118.0 %all-reduce.2.cloned.1.call-done = bf16[8,3,4096]{2,0,1:T(8,128)(2,1)} async-done(((bf16[8,3,4096]{2,0,1:T(8,128)(2,1)}), bf16[8,3,4096]{2,0,1:T(8,128)(2,1)}) %all-reduce.2.cloned.1.call-update) | async-done | bytes 196624 | tf_op jit(solution)/shard_map/psum | solution.py:16
  127.7 1.0 convert_element_type.34
  129.4 1.1 fusion.46
  130.6 1.1 fusion.43
  131.7 3.8 %fusion.48 = (f32[64,3,4032]{2,0,1:T(8,128)}, f32[64,3,4032]{2,0,1:T(8,128)}) fusion(f32[64,3,4096]{2,0,1:T(8,128)S(1)} %get-tuple-element.53), kind=kLoop, calls=%fused_computation.65 | loop fusion | bytes 12386304 | tf_op jit(solution)/shard_map/jit(_roll_static)/slice | solution.py:37
  135.6 1.4 collective-permute-start
  137.0 4.4 %collective-permute-start.1 = (bf16[64,1,4096]{2,0,1:T(8,128)(2,1)S(1)}, bf16[64,1,4096]{2,0,1:T(8,128)(2,1)S(1)}, u32[]{:S(2)}, u32[]{:S(2)}) collective-permute-start(bf16[64,1,4096]{2,0,1:T(8,128)(2,1)S(1)} %get-tuple-element.51), channel_id=1, source_target_pairs={{1,0},{2,1},{3,2},{4,3},{5,4},{6,5},{7,6},{8,7},{9,8},{10,9},{11,1... | collective-permute-start | bytes 1572872 | tf_op jit(solution)/shard_map/ppermute | solution.py:28
  141.4 0.7 fusion.47
  142.1 0.7 fusion.45
  142.8 0.7 fusion.44
  143.6 10.0 %collective-permute-done = bf16[64,1,4096]{2,0,1:T(8,128)(2,1)S(1)} collective-permute-done((bf16[64,1,4096]{2,0,1:T(8,128)(2,1)S(1)}, bf16[64,1,4096]{2,0,1:T(8,128)(2,1)S(1)}, u32[]{:S(2)}, u32[]{:S(2)}) %collective-permute-start) | collective-permute-done | bytes 524320 | tf_op jit(solution)/shard_map/ppermute | solution.py:25
  154.0 7.2 %fusion.29 = (bf16[64,3,4096]{2,0,1:T(8,128)(2,1)}, f32[64,3,4096]{2,0,1:T(8,128)S(1)}) fusion(f32[64,3,64]{2,0,1:T(8,128)} %get-tuple-element.43, f32[64,3,4032]{2,0,1:T(8,128)} %get-tuple-element.45, f32[64,3,4032]{2,0,1:T(8,128)} %get-tuple-element.44, f32[64,3,64]{2,0,1:T(8,128)} %get-tuple-element.42, f32[64,3,1]{2,0,1:T(8,128)} %get-tuple-element.39, ...), kind=kLoop, calls=%fused_computation.47 | loop fusion | flops 13369344 | bytes 30679040 | tf_op jit(solution)/shard_map/convert_element_type | solution.py:55
  161.2 1.1 fusion.40
  162.4 3.0 %fusion.37 = (f32[64,3,4033]{2,0,1:T(8,128)S(1)}, f32[64,3,4033]{2,0,1:T(8,128)}) fusion(f32[64,3,4096]{2,0,1:T(8,128)S(1)} %get-tuple-element.9), kind=kLoop, calls=%fused_computation.54 | loop fusion | bytes 12389376 | tf_op jit(solution)/shard_map/jit(_roll_static)/slice | solution.py:35
  165.3 3.8 %fusion.42 = (f32[64,3,4032]{2,0,1:T(8,128)}, f32[64,3,4032]{2,0,1:T(8,128)}) fusion(f32[64,3,4096]{2,0,1:T(8,128)S(1)} %get-tuple-element.9), kind=kLoop, calls=%fused_computation.59 | loop fusion | bytes 12386304 | tf_op jit(solution)/shard_map/jit(_roll_static)/slice | solution.py:37
  169.5 5.9 %collective-permute-start.3 = (bf16[64,1,4096]{2,0,1:T(8,128)(2,1)S(1)}, bf16[64,1,4096]{2,0,1:T(8,128)(2,1)S(1)}, u32[]{:S(2)}, u32[]{:S(2)}) collective-permute-start(bf16[64,1,4096]{2,0,1:T(8,128)(2,1)S(1)} %get-tuple-element.49), channel_id=1, source_target_pairs={{1,0},{2,1},{3,2},{4,3},{5,4},{6,5},{7,6},{8,7},{9,8},{10,9},{11,1... | collective-permute-start | bytes 1572872 | tf_op jit(solution)/shard_map/ppermute | solution.py:28
  175.5 0.7 fusion.41
  176.2 0.7 fusion.39
  177.7 10.0 %collective-permute-done.2 = bf16[64,1,4096]{2,0,1:T(8,128)(2,1)S(1)} collective-permute-done((bf16[64,1,4096]{2,0,1:T(8,128)(2,1)S(1)}, bf16[64,1,4096]{2,0,1:T(8,128)(2,1)S(1)}, u32[]{:S(2)}, u32[]{:S(2)}) %collective-permute-start.2) | collective-permute-done | bytes 524320 | tf_op jit(solution)/shard_map/ppermute | solution.py:25
  188.1 6.6 %fusion.27 = (bf16[64,3,4096]{2,0,1:T(8,128)(2,1)S(1)}, f32[64,3,4096]{2,0,1:T(8,128)S(1)}) fusion(f32[64,3,64]{2,0,1:T(8,128)S(1)} %copy-done.7, f32[64,3,4032]{2,0,1:T(8,128)} %get-tuple-element.33, f32[64,3,4032]{2,0,1:T(8,128)} %get-tuple-element.32, f32[64,3,64]{2,0,1:T(8,128)S(1)} %copy-done.6, f32[64,3,1]{2,0,1:T(8,128)} %get-tuple-element.27, ...), kind=kLoop, calls=%fused_computation.46 | loop fusion | flops 13369344 | bytes 30679040 | tf_op jit(solution)/shard_map/convert_element_type | solution.py:55
  194.7 1.1 fusion.31
  195.9 1.1 fusion.33
  197.1 1.1 fusion.36
  198.4 5.6 %collective-permute-start.5 = (bf16[64,1,4096]{2,0,1:T(8,128)(2,1)S(1)}, bf16[64,1,4096]{2,0,1:T(8,128)(2,1)S(1)}, u32[]{:S(2)}, u32[]{:S(2)}) collective-permute-start(bf16[64,1,4096]{2,0,1:T(8,128)(2,1)S(1)} %get-tuple-element.47), channel_id=1, source_target_pairs={{1,0},{2,1},{3,2},{4,3},{5,4},{6,5},{7,6},{8,7},{9,8},{10,9},{11,1... | collective-permute-start | bytes 1572872 | tf_op jit(solution)/shard_map/ppermute | solution.py:28
  204.0 0.7 fusion.35
  206.2 9.3 %collective-permute-done.4 = bf16[64,1,4096]{2,0,1:T(8,128)(2,1)S(1)} collective-permute-done((bf16[64,1,4096]{2,0,1:T(8,128)(2,1)S(1)}, bf16[64,1,4096]{2,0,1:T(8,128)(2,1)S(1)}, u32[]{:S(2)}, u32[]{:S(2)}) %collective-permute-start.4) | collective-permute-done | bytes 524320 | tf_op jit(solution)/shard_map/ppermute | solution.py:25
  215.5 1.8 maximum_convert_fusion.2
  217.3 5.9 %fusion.5 = f32[8,3,4096]{2,0,1:T(8,128)} fusion(f32[64,5,4096]{2,0,1:T(8,128)S(1)} %maximum_convert_fusion.2, f32[64,3,63]{2,0,1:T(8,128)} %get-tuple-element.19, f32[64,3,4033]{2,0,1:T(8,128)S(1)} %get-tuple-element.21, f32[64,3,4095]{2,0,1:T(8,128)S(1)} %get-tuple-element.15, f32[64,3,1]{2,0,1:T(8,128)} %get-tuple-element.17, ...), kind=kLoop, calls=%fused_computation.6 | loop fusion | flops 14057472 | bytes 26353664 | tf_op jit(solution)/shard_map/reduce_sum | solution.py:59
  223.2 1.0 negate_convert_fusion
  224.3 1.2 convolution_bitcast_fusion
  225.5 42.0 %psum.15 = f32[8,8]{0,1:T(8,128)S(1)} all-reduce(f32[8,8]{0,1:T(8,128)S(1)} %convolution_bitcast_fusion), channel_id=1, replica_groups=mesh['orb'=16,'dom'=16] {'dom'}, use_global_device_ids=true, to_apply=%region_2.3 | all-reduce | flops 64 | bytes 512 | tf_op jit(solution)/shard_map/psum | solution.py:65
  (39 shorter events, 5.1 us)
Async XLA Ops:
  7.2 120.5 %all-reduce.2.cloned.1.call-start = ((), (), s32[]{:S(2)}) async-start(), calls=%async_computation | async-start | bytes 393216 | tf_op jit(solution)/shard_map/psum | solution.py:16
  9.6 119.6 %copy-start.4 = (f32[8,3,4096]{2,0,1:T(8,128)}, f32[8,3,4096]{2,0,1:T(8,128)S(1)}, u32[]{:S(2)}) copy-start(f32[8,3,4096]{2,0,1:T(8,128)S(1)} %get-tuple-element.55) | copy-start | bytes 1179652
  9.6 144.3 %copy-start.8 = (pred[4096]{0:T(1024)(128)(4,1)}, pred[4096]{0:T(1024)(128)(4,1)S(1)}, u32[]{:S(2)}) copy-start(pred[4096]{0:T(1024)(128)(4,1)S(1)} %get-tuple-element.57) | copy-start | bytes 12292
  128.7 0.7 copy-start.2
  135.6 17.9 %collective-permute-start = (bf16[64,1,4096]{2,0,1:T(8,128)(2,1)S(1)}, bf16[64,1,4096]{2,0,1:T(8,128)(2,1)S(1)}, u32[]{:S(2)}, u32[]{:S(2)}) collective-permute-start(bf16[64,1,4096]{2,0,1:T(8,128)(2,1)S(1)} %get-tuple-element.50), channel_id=1, source_target_pairs={{0,1},{1,2},{2,3},{3,4},{4,5},{5,6},{6,7},{7,8},{8,9},{9,10},{10,1... | collective-permute-start | bytes 1572872 | tf_op jit(solution)/shard_map/ppermute | solution.py:25
  137.0 16.6 %collective-permute-start.1 = (bf16[64,1,4096]{2,0,1:T(8,128)(2,1)S(1)}, bf16[64,1,4096]{2,0,1:T(8,128)(2,1)S(1)}, u32[]{:S(2)}, u32[]{:S(2)}) collective-permute-start(bf16[64,1,4096]{2,0,1:T(8,128)(2,1)S(1)} %get-tuple-element.51), channel_id=1, source_target_pairs={{1,0},{2,1},{3,2},{4,3},{5,4},{6,5},{7,6},{8,7},{9,8},{10,9},{11,1... | collective-permute-start | bytes 1572872 | tf_op jit(solution)/shard_map/ppermute | solution.py:28
  165.3 3.8 %copy-start = (bf16[64,3,4096]{2,0,1:T(8,128)(2,1)S(1)}, bf16[64,3,4096]{2,0,1:T(8,128)(2,1)}, u32[]{:S(2)}) copy-start(bf16[64,3,4096]{2,0,1:T(8,128)(2,1)} %get-tuple-element.8) | copy-start | bytes 4718596
  169.3 18.4 %collective-permute-start.2 = (bf16[64,1,4096]{2,0,1:T(8,128)(2,1)S(1)}, bf16[64,1,4096]{2,0,1:T(8,128)(2,1)S(1)}, u32[]{:S(2)}, u32[]{:S(2)}) collective-permute-start(bf16[64,1,4096]{2,0,1:T(8,128)(2,1)S(1)} %get-tuple-element.48), channel_id=1, source_target_pairs={{0,1},{1,2},{2,3},{3,4},{4,5},{5,6},{6,7},{7,8},{8,9},{9,10},{10,1... | collective-permute-start | bytes 1572872 | tf_op jit(solution)/shard_map/ppermute | solution.py:25
  169.5 18.1 %collective-permute-start.3 = (bf16[64,1,4096]{2,0,1:T(8,128)(2,1)S(1)}, bf16[64,1,4096]{2,0,1:T(8,128)(2,1)S(1)}, u32[]{:S(2)}, u32[]{:S(2)}) collective-permute-start(bf16[64,1,4096]{2,0,1:T(8,128)(2,1)S(1)} %get-tuple-element.49), channel_id=1, source_target_pairs={{1,0},{2,1},{3,2},{4,3},{5,4},{6,5},{7,6},{8,7},{9,8},{10,9},{11,1... | collective-permute-start | bytes 1572872 | tf_op jit(solution)/shard_map/ppermute | solution.py:28
  177.7 10.4 %copy-start.3 = (f32[8,3,4096]{2,0,1:T(8,128)S(1)}, f32[8,3,4096]{2,0,1:T(8,128)}, u32[]{:S(2)}) copy-start(f32[8,3,4096]{2,0,1:T(8,128)} %copy-done.2) | copy-start | bytes 1179652
  177.7 10.4 %copy-start.6 = (f32[64,3,64]{2,0,1:T(8,128)S(1)}, f32[64,3,64]{2,0,1:T(8,128)}, u32[]{:S(2)}) copy-start(f32[64,3,64]{2,0,1:T(8,128)} %get-tuple-element.30) | copy-start | bytes 147460
  177.7 10.4 %copy-start.7 = (f32[64,3,64]{2,0,1:T(8,128)S(1)}, f32[64,3,64]{2,0,1:T(8,128)}, u32[]{:S(2)}) copy-start(f32[64,3,64]{2,0,1:T(8,128)} %get-tuple-element.31) | copy-start | bytes 147460
  194.7 3.5 %copy-start.1 = (bf16[64,3,4096]{2,0,1:T(8,128)(2,1)}, bf16[64,3,4096]{2,0,1:T(8,128)(2,1)S(1)}, u32[]{:S(2)}) copy-start(bf16[64,3,4096]{2,0,1:T(8,128)(2,1)S(1)} %get-tuple-element.6) | copy-start | bytes 4718596
  198.3 17.2 %collective-permute-start.4 = (bf16[64,1,4096]{2,0,1:T(8,128)(2,1)S(1)}, bf16[64,1,4096]{2,0,1:T(8,128)(2,1)S(1)}, u32[]{:S(2)}, u32[]{:S(2)}) collective-permute-start(bf16[64,1,4096]{2,0,1:T(8,128)(2,1)S(1)} %get-tuple-element.46), channel_id=1, source_target_pairs={{0,1},{1,2},{2,3},{3,4},{4,5},{5,6},{6,7},{7,8},{8,9},{9,10},{10,1... | collective-permute-start | bytes 1572872 | tf_op jit(solution)/shard_map/ppermute | solution.py:25
  198.4 17.1 %collective-permute-start.5 = (bf16[64,1,4096]{2,0,1:T(8,128)(2,1)S(1)}, bf16[64,1,4096]{2,0,1:T(8,128)(2,1)S(1)}, u32[]{:S(2)}, u32[]{:S(2)}) collective-permute-start(bf16[64,1,4096]{2,0,1:T(8,128)(2,1)S(1)} %get-tuple-element.47), channel_id=1, source_target_pairs={{1,0},{2,1},{3,2},{4,3},{5,4},{6,5},{7,6},{8,7},{9,8},{10,9},{11,1... | collective-permute-start | bytes 1572872 | tf_op jit(solution)/shard_map/ppermute | solution.py:28
  206.2 11.1 %copy-start.9 = (pred[4096]{0:T(1024)(128)(4,1)S(1)}, pred[4096]{0:T(1024)(128)(4,1)}, u32[]{:S(2)}) copy-start(pred[4096]{0:T(1024)(128)(4,1)} %copy-done.8) | copy-start | bytes 12292
  224.3 43.9 %copy-start.5 = (bf16[8,3,4096]{2,0,1:T(8,128)(2,1)}, bf16[8,3,4096]{2,0,1:T(8,128)(2,1)S(1)}, u32[]{:S(2)}) copy-start(bf16[8,3,4096]{2,0,1:T(8,128)(2,1)S(1)} %negate_convert_fusion) | copy-start | bytes 589828
Sparse Core Ops, SparseCore 0:
  11.2 116.4 all-reduce.1
where the time goes:
time: 275 us
  waiting for transfers between devices  147 us (53%)
  blocking collectives  42 us (15%)
  other arithmetic  26.7 us (10%)
  local copies, waits for them, and re-layouts  25.2 us (9%)
  starting transfers between devices  17.7 us (6%)
  between operations  14.9 us (5%)
    psum x1, waiting for transfers between devices, broadcast(): return lax.psum(block, axis)  118 us
    psum x1, blocking collectives, on_device(): total = lax.psum(partial_prod, 'dom') / 512.0  42 us
    ppermute x3, waiting for transfers between devices, with_halo(): lax.ppermute(lax.slice_in_dim(block, block.shape[dim] - width, None, axis...  29.2 us
    ppermute x3, starting transfers between devices, with_halo(): lax.ppermute(lax.slice_in_dim(block, 0, width, axis=dim), axis, backward)  15.9 us
    convert_element_type x3, other arithmetic, on_device(): pot.astype(jnp.bfloat16)  14.4 us
    slice x6, local copies, waits for them, and re-layouts, plane_sum(): return lower + upper + jnp.roll(field, NY, -1) + jnp.roll(field, -NY, -1)  11 us
    reduce_sum x1, other arithmetic, on_device(): applied = (-jnp.sum(pot * phif[:, None], axis=0)).astype(jnp.bfloat16)  5.93 us
    slice x4, local copies, waits for them, and re-layouts, plane_sum(): jnp.roll(field, 1 - NY, -1)  5.57 us
  transfers between devices with their start and end apart: 7, of which 4 were waited for; matrix products, arithmetic and copies ran while one was open for 2% of the time, Pallas kernels for 0%

commit v1 on v0

v1 whole, which is shorter than its diff:
```python
import itertools

import jax
import jax.numpy as jnp
from jax import lax
from jax.experimental import pallas as pl
from jax.experimental.pallas import tpu as pltpu
from jax.sharding import PartitionSpec as P

NY = 64
OWN = 8
LANES = 128
ROWS = 32
PAD = 2
DEPTH = 3
REACH = 3

C = 1.0 / 6.02


def weight(dx, dy, dz):
    steps = ((1, 0, 0), (-1, 0, 0), (0, 1, 0), (0, -1, 0), (0, 0, 1), (0, 0, -1))
    total = 0.0
    for length in range(REACH + 1):
        walks = sum(
            tuple(map(sum, zip((0, 0, 0), *walk))) == (dx, dy, dz)
            for walk in itertools.product(steps, repeat=length)
        )
        total += walks * C ** (length + 1)
    return total


WEIGHTS = {
    d: weight(*d)
    for d in itertools.product(range(REACH + 1), repeat=3)
    if sum(d) <= REACH
}


def spread_matrix():
    row = lax.broadcasted_iota(jnp.int32, (LANES, 2 * LANES), 0)
    col = lax.broadcasted_iota(jnp.int32, (LANES, 2 * LANES), 1)
    half = col // LANES
    lane = col % LANES
    source = (lane % 2 + half) % 2 * NY + lane // 2
    return jnp.where(row == source, 1.0, 0.0).astype(jnp.bfloat16)


def gather_matrix():
    row = lax.broadcasted_iota(jnp.int32, (LANES, LANES), 0)
    col = lax.broadcasted_iota(jnp.int32, (LANES, LANES), 1)
    source = col % NY * 2 + col // NY
    return jnp.where(row == source, 1.0, 0.0).astype(jnp.bfloat16)


def kernel(phi_m, phi_0, phi_p, orb_m, orb_0, orb_p, out, part, fa, fb, oa, ob, acc):
    spread = spread_matrix()
    odd = lax.broadcasted_iota(jnp.int32, (ROWS * OWN, LANES), 1) % 2 == 1

    def lay_out(source, even_ref, odd_ref, plane):
        wide = source.astype(jnp.float32)
        tall = jnp.concatenate(
            [wide[:, r * LANES : (r + 1) * LANES] for r in range(ROWS)], axis=0
        )
        both = jnp.dot(
            tall.astype(jnp.bfloat16), spread, preferred_element_type=jnp.float32
        )
        a, b = both[:, :LANES], both[:, LANES:]
        b = jnp.where(odd, jnp.concatenate([b[OWN:], b[:OWN]], axis=0), b)
        n, p = ROWS * OWN, PAD * OWN
        for ref, value in ((even_ref, a), (odd_ref, b)):
            ref[plane, p : p + n] = value
            ref[plane, :p] = value[n - p :]
            ref[plane, p + n :] = value[:p]

    for block, (f, o) in enumerate(((phi_m, orb_m), (phi_0, orb_0), (phi_p, orb_p))):
        for z in range(DEPTH):
            lay_out(f[z], fa, fb, block * DEPTH + z)
            lay_out(o[z], oa, ob, block * DEPTH + z)

    def plane_step(z, carry):
        for tile in range(ROWS // 8):

            def read(refs, dx, dz, i):
                ref, k = refs[dx % 2], dx // 2
                start = (tile * 8 + PAD + k) * OWN + i
                return ref[z + (DEPTH + dz), pl.ds(start, 8, stride=OWN), :]

            total = [None] * OWN
            for dy in range(-REACH, REACH + 1):
                here = [read((fa, fb), 0, 0, i) for i in range(OWN)]
                if dy:
                    here = [pltpu.roll(v, 2 * dy % LANES, 1) for v in here]
                sums = [None] * OWN
                rest = REACH - abs(dy)
                for dz in range(-rest, rest + 1):
                    for dx in range(abs(dz) - rest, rest - abs(dz) + 1):
                        g = None
                        for i in range(OWN):
                            term = here[i] * read((fa, fb), dx, dz, i)
                            g = term if g is None else g + term
                        g = g * (-WEIGHTS[abs(dx), abs(dy), abs(dz)])
                        for j in range(OWN):
                            term = g * read((oa, ob), dx, dz, j)
                            sums[j] = term if sums[j] is None else sums[j] + term
                for j in range(OWN):
                    s = pltpu.roll(sums[j], -2 * dy % LANES, 1) if dy else sums[j]
                    total[j] = s if total[j] is None else total[j] + s
            for j in range(OWN):
                acc[z, pl.ds(tile * 8 * OWN + j, 8, stride=OWN), :] = total[j]
        return carry

    lax.fori_loop(0, DEPTH, plane_step, 0)

    gather = gather_matrix()
    products = None
    for z in range(DEPTH):
        tall = jnp.dot(
            acc[z].astype(jnp.bfloat16), gather, preferred_element_type=jnp.float32
        )
        wide = jnp.concatenate(
            [tall[r * OWN : (r + 1) * OWN] for r in range(ROWS)], axis=1
        ).astype(jnp.bfloat16)
        out[z] = wide
        term = lax.dot_general(
            orb_0[z], wide, (((1,), (1,)), ((), ())), preferred_element_type=jnp.float32
        )
        products = term if products is None else products + term
    part[...] = products


def apply_exchange(phis, orbs):
    rows = (ROWS + 2 * PAD) * OWN
    field = pltpu.VMEM((3 * DEPTH, rows, LANES), jnp.float32)
    return pl.pallas_call(
        kernel,
        out_shape=(
            jax.ShapeDtypeStruct((DEPTH, OWN, ROWS * LANES), jnp.bfloat16),
            jax.ShapeDtypeStruct((OWN, OWN), jnp.float32),
        ),
        in_specs=[pl.BlockSpec(memory_space=pltpu.VMEM)] * 6,
        out_specs=[pl.BlockSpec(memory_space=pltpu.VMEM)] * 2,
        scratch_shapes=[field] * 4
        + [pltpu.VMEM((DEPTH, ROWS * OWN, LANES), jnp.float32)],
        compiler_params=pltpu.CompilerParams(vmem_limit_bytes=40 * 1024 * 1024),
        cost_estimate=pl.CostEstimate(
            flops=50_000_000, bytes_accessed=2_000_000, transcendentals=0
        ),
    )(*phis, *orbs)


def halo(x, pairs_of):
    return lax.ppermute(x, ("orb", "dom"), pairs_of(1)), lax.ppermute(
        x, ("orb", "dom"), pairs_of(-1)
    )


def slab_pairs(groups, count):
    return lambda step: [
        (g * count + s, g * count + (s + step) % count)
        for g in groups
        for s in range(count)
    ]


def phi_from(owner, count, x):
    me = lax.axis_index("orb")
    have = [owner]
    buf = jnp.where(me == owner, x, 0)
    for bit in (2, 6, 8):
        buf = buf + lax.ppermute(buf, "orb", [(h, h ^ bit) for h in have])
        have = have + [h ^ bit for h in have]
    low, high = halo(buf, slab_pairs(have, count))
    full = jnp.concatenate([low, buf, high], axis=0)
    return full + lax.ppermute(full, "orb", [(h, h ^ 1) for h in range(16)])


def on_device(orbitals, block_owner):
    count = lax.axis_size("dom")
    groups = lax.axis_size("orb")
    x = jnp.transpose(orbitals, (1, 0, 2))
    low, high = halo(x, slab_pairs(range(groups), count))
    phi = lax.switch(
        block_owner[0],
        [lambda v, w=w: phi_from(w, count, v) for w in range(groups)],
        x,
    )
    phis = (phi[:DEPTH], phi[DEPTH : 2 * DEPTH], phi[2 * DEPTH :])
    applied, total = apply_exchange(phis, (low, x, high))
    for bits in (1, 3, 6, 8):
        total = total + lax.ppermute(
            total, "dom", [(s, s ^ bits) for s in range(count)]
        )
    return jnp.transpose(applied, (1, 0, 2)), total / 512.0


def solution(mesh):
    in_specs = (P("orb", "dom", None), P())
    out_specs = (P("orb", "dom", None), P("orb", None))
    return jax.shard_map(
        on_device, mesh=mesh, in_specs=in_specs, out_specs=out_specs, check_vma=False
    )
```

time: 275 us -> 98.9 us (0.36)
  the two profiles are of different devices: /device:TPU:16 before, /device:TPU:1 now
where the time goes in v1:
time: 98.9 us; the launch traced here: 101 us
  starting transfers between devices  70.8 us (72%)
  waiting for transfers between devices  14.9 us (15%)
  Pallas kernels  10 us (10%)
  other arithmetic  1.74 us (2%)
  between operations  1.31 us (1%)
  local copies, waits for them, and re-layouts  1.22 us (1%)
    ppermute x1, starting transfers between devices, phi_from(): return full + lax.ppermute(full, 'orb', [(h, h ^ 1) for h in range(16)])  30.8 us
    ppermute x4, starting transfers between devices, on_device(): lax.ppermute(total, 'dom', [(s, s ^ bits) for s in range(count)])  21.7 us
    ppermute x4, waiting for transfers between devices, on_device(): lax.ppermute(total, 'dom', [(s, s ^ bits) for s in range(count)])  13.3 us
    ppermute x2, starting transfers between devices, halo(): lax.ppermute(x, ('orb', 'dom'), pairs_of(-1))  13 us
    pallas_call x1, Pallas kernels, apply_exchange(): pl.pallas_call(kernel, out_shape=(jax.ShapeDtypeStruct((DEPTH, OWN, ROWS...  10 us
    ppermute x2, starting transfers between devices, halo(): lax.ppermute(x, ('orb', 'dom'), pairs_of(1))  3.22 us
    ppermute x3, starting transfers between devices, phi_from(): buf = buf + lax.ppermute(buf, 'orb', [(h, h ^ bit) for h in have])  2.15 us
  transfers between devices with their start and end apart: 12, of which 5 were waited for; matrix products, arithmetic and copies ran while one was open for 2% of the time, Pallas kernels for 0%

profile of v1, /device:TPU:1, one launch (start us, length us, event | category | flops | bytes accessed | tf_op | source)
XLA Modules:
  0.0 100.6 jit_solution(11658705275026297832)
XLA Ops:
  0.6 2.5 %collective-permute-start.96 = (bf16[3,8,4096]{2,1,0:T(8,128)(2,1)}, bf16[3,8,4096]{2,1,0:T(8,128)(2,1)S(1)}, u32[]{:S(2)}, u32[]{:S(2)}) collective-permute-start(bf16[3,8,4096]{2,1,0:T(8,128)(2,1)} %bitcast.3), channel_id=1, source_target_pairs={{0,1},{1,2},{2,3},{3,4},{4,5},{5,6},{6,7},{7,8},{8,9},{9,10},{10,1... | collective-permute-start | bytes 589832 | tf_op jit(solution)/shard_map/ppermute | solution.py:153
  3.2 12.3 %collective-permute-start.97 = (bf16[3,8,4096]{2,1,0:T(8,128)(2,1)}, bf16[3,8,4096]{2,1,0:T(8,128)(2,1)S(1)}, u32[]{:S(2)}, u32[]{:S(2)}) collective-permute-start(bf16[3,8,4096]{2,1,0:T(8,128)(2,1)} %bitcast.4), channel_id=1, source_target_pairs={{0,15},{1,0},{2,1},{3,2},{4,3},{5,4},{6,5},{7,6},{8,7},{9,8},{10,9... | collective-permute-start | bytes 589832 | tf_op jit(solution)/shard_map/ppermute | solution.py:153
  16.2 38.8 %conditional.1 = (bf16[9,8,4096]{2,1,0:T(8,128)(2,1)}, bf16[3,8,4096]{2,1,0:T(8,128)(2,1)S(1)}, bf16[3,8,4096]{2,1,0:T(8,128)(2,1)S(1)}, bf16[3,8,4096]{2,1,0:T(8,128)(2,1)S(1)}) conditional(s32[]{:T(128)} %bitcast, bf16[3,8,4096]{2,1,0:T(8,128)(2,1)} %bitcast.5, bf16[3,8,4096]{2,1,0:T(8,128)(2,1)} %bitcast.6, ...), branch_computations={%region_0.1_spmd, %region_1.2_spmd, %region_2.3_spmd, %region_3.4_... | conditional | flops 1966084 | bytes 13369687 | solution.py:183
  16.4 0.0 copy-start.14
  16.4 0.8 collective-permute-start.84
  17.3 0.0 collective-permute-done.84
  17.3 0.1 copy-done.14
  17.4 0.7 collective-permute-start.85
  18.0 0.0 collective-permute-done.85
  18.1 0.7 collective-permute-start.86
  18.8 0.0 collective-permute-done.86
  18.9 0.7 collective-permute-start.87
  19.5 0.7 collective-permute-start.88
  20.2 0.0 collective-permute-done.87
  20.2 0.0 collective-permute-done.88
  20.2 0.1 pad_maximum_fusion.14
  20.3 30.8 %collective-permute-start.89 = (bf16[9,8,4096]{2,1,0:T(8,128)(2,1)S(1)}, bf16[9,8,4096]{2,1,0:T(8,128)(2,1)S(1)}, u32[]{:S(2)}, u32[]{:S(2)}) collective-permute-start(bf16[9,8,4096]{2,1,0:T(8,128)(2,1)S(1)} %pad_maximum_fusion.14), channel_id=1, source_target_pairs={{0,16},{16,0},{32,48},{48,32},{64,80},{80,64},{96,112},{112,96},{1... | collective-permute-start | bytes 1769480 | tf_op jit(solution)/shard_map/cond/branch_14_fun/ppermute | solution.py:175
  51.1 1.6 %collective-permute-done.89 = bf16[9,8,4096]{2,1,0:T(8,128)(2,1)S(1)} collective-permute-done((bf16[9,8,4096]{2,1,0:T(8,128)(2,1)S(1)}, bf16[9,8,4096]{2,1,0:T(8,128)(2,1)S(1)}, u32[]{:S(2)}, u32[]{:S(2)}) %collective-permute-start.89) | collective-permute-done | bytes 589856 | tf_op jit(solution)/shard_map/cond/branch_14_fun/ppermute | solution.py:175
  52.7 0.9 fusion.14
  53.6 1.2 %fusion.30 = (bf16[3,8,4096]{2,1,0:T(8,128)(2,1)S(1)}, bf16[3,8,4096]{2,1,0:T(8,128)(2,1)S(1)}, bf16[3,8,4096]{2,1,0:T(8,128)(2,1)S(1)}) fusion(bf16[9,8,4096]{2,1,0:T(8,128)(2,1)} %fusion.14), kind=kLoop, calls=%fused_computation.63 | loop fusion | bytes 1179648 | tf_op jit(solution)/shard_map/slice | solution.py:188
  55.0 0.0 collective-permute-done.96.orb_m
  55.0 0.0 collective-permute-done.97.orb_p
  55.0 10.0 %shard_map.41 = (bf16[3,8,4096]{2,1,0:T(8,128)(2,1)}, f32[8,8]{1,0:T(8,128)S(1)}) custom-call(bf16[3,8,4096]{2,1,0:T(8,128)(2,1)S(1)} %get-tuple-element.27.phi_m, bf16[3,8,4096]{2,1,0:T(8,128)(2,1)S(1)} %get-tuple-element.28.phi_0, bf16[3,8,4096]{2,1,0:T(8,128)(2,1)S(1)} %get-tuple-element.29.phi_p, bf16[3,8,4096]{2,1,0:T(8,128)(2,1)S(1)} %collective-permute-done.96.orb_m, ...), custom_call_target="tpu_custom_call" | custom-call | flops 50000000 | bytes 2000000 | tf_op jit(solution)/shard_map/pallas_call | solution.py:135
  65.1 0.0 collective-permute-start.98
  65.1 2.5 %collective-permute-done.98 = f32[8,8]{1,0:T(8,128)S(1)} collective-permute-done((f32[8,8]{1,0:T(8,128)S(1)}, f32[8,8]{1,0:T(8,128)S(1)}, u32[]{:S(2)}, u32[]{:S(2)}) %collective-permute-start.98) | collective-permute-done | bytes 288 | tf_op jit(solution)/shard_map/ppermute | solution.py:191
  67.5 3.7 %collective-permute-start.99 = (f32[8,8]{1,0:T(8,128)S(1)}, f32[8,8]{1,0:T(8,128)S(1)}, u32[]{:S(2)}, u32[]{:S(2)}) collective-permute-start(f32[8,8]{1,0:T(8,128)S(1)} %add.204), channel_id=1, source_target_pairs={{0,3},{1,2},{2,1},{3,0},{4,7},{5,6},{6,5},{7,4},{8,11},{9,10},{10,... | collective-permute-start | bytes 776 | tf_op jit(solution)/shard_map/ppermute | solution.py:191
  71.2 1.0 collective-permute-done.99
  72.2 9.7 %collective-permute-start.100 = (f32[8,8]{1,0:T(8,128)S(1)}, f32[8,8]{1,0:T(8,128)S(1)}, u32[]{:S(2)}, u32[]{:S(2)}) collective-permute-start(f32[8,8]{1,0:T(8,128)S(1)} %add.205), channel_id=1, source_target_pairs={{0,6},{1,7},{2,4},{3,5},{4,2},{5,3},{6,0},{7,1},{8,14},{9,15},{10,... | collective-permute-start | bytes 776 | tf_op jit(solution)/shard_map/ppermute | solution.py:191
  81.9 6.0 %collective-permute-done.100 = f32[8,8]{1,0:T(8,128)S(1)} collective-permute-done((f32[8,8]{1,0:T(8,128)S(1)}, f32[8,8]{1,0:T(8,128)S(1)}, u32[]{:S(2)}, u32[]{:S(2)}) %collective-permute-start.100) | collective-permute-done | bytes 288 | tf_op jit(solution)/shard_map/ppermute | solution.py:191
  87.9 8.3 %collective-permute-start.101 = (f32[8,8]{1,0:T(8,128)S(1)}, f32[8,8]{1,0:T(8,128)S(1)}, u32[]{:S(2)}, u32[]{:S(2)}) collective-permute-start(f32[8,8]{1,0:T(8,128)S(1)} %add.206), channel_id=1, source_target_pairs={{0,8},{1,9},{2,10},{3,11},{4,12},{5,13},{6,14},{7,15},{8,0},{9,1},... | collective-permute-start | bytes 776 | tf_op jit(solution)/shard_map/ppermute | solution.py:191
  96.1 3.9 %collective-permute-done.101 = f32[8,8]{1,0:T(8,128)S(1)} collective-permute-done((f32[8,8]{1,0:T(8,128)S(1)}, f32[8,8]{1,0:T(8,128)S(1)}, u32[]{:S(2)}, u32[]{:S(2)}) %collective-permute-start.101) | collective-permute-done | bytes 288 | tf_op jit(solution)/shard_map/ppermute | solution.py:191
  100.0 0.6 add_multiply_fusion
  (7 shorter events, 0.2 us)
Async XLA Ops:
  0.6 54.4 %collective-permute-start.96 = (bf16[3,8,4096]{2,1,0:T(8,128)(2,1)}, bf16[3,8,4096]{2,1,0:T(8,128)(2,1)S(1)}, u32[]{:S(2)}, u32[]{:S(2)}) collective-permute-start(bf16[3,8,4096]{2,1,0:T(8,128)(2,1)} %bitcast.3), channel_id=1, source_target_pairs={{0,1},{1,2},{2,3},{3,4},{4,5},{5,6},{6,7},{7,8},{8,9},{9,10},{10,1... | collective-permute-start | bytes 589832 | tf_op jit(solution)/shard_map/ppermute | solution.py:153
  3.2 51.8 %collective-permute-start.97 = (bf16[3,8,4096]{2,1,0:T(8,128)(2,1)}, bf16[3,8,4096]{2,1,0:T(8,128)(2,1)S(1)}, u32[]{:S(2)}, u32[]{:S(2)}) collective-permute-start(bf16[3,8,4096]{2,1,0:T(8,128)(2,1)} %bitcast.4), channel_id=1, source_target_pairs={{0,15},{1,0},{2,1},{3,2},{4,3},{5,4},{6,5},{7,6},{8,7},{9,8},{10,9... | collective-permute-start | bytes 589832 | tf_op jit(solution)/shard_map/ppermute | solution.py:153
  16.4 0.9 copy-start.14
  16.4 0.8 collective-permute-start.84
  17.4 0.7 collective-permute-start.85
  18.1 0.7 collective-permute-start.86
  18.9 1.4 %collective-permute-start.87 = (bf16[3,8,4096]{2,1,0:T(8,128)(2,1)S(1)}, bf16[3,8,4096]{2,1,0:T(8,128)(2,1)S(1)}, u32[]{:S(2)}, u32[]{:S(2)}) collective-permute-start(bf16[3,8,4096]{2,1,0:T(8,128)(2,1)S(1)} %add.194), channel_id=1, source_target_pairs={{224,225},{225,226},{226,227},{227,228},{228,229},{229,230},{230,2... | collective-permute-start | bytes 589832 | tf_op jit(solution)/shard_map/cond/branch_14_fun/ppermute | solution.py:153
  19.5 0.7 collective-permute-start.88
  20.3 32.4 %collective-permute-start.89 = (bf16[9,8,4096]{2,1,0:T(8,128)(2,1)S(1)}, bf16[9,8,4096]{2,1,0:T(8,128)(2,1)S(1)}, u32[]{:S(2)}, u32[]{:S(2)}) collective-permute-start(bf16[9,8,4096]{2,1,0:T(8,128)(2,1)S(1)} %pad_maximum_fusion.14), channel_id=1, source_target_pairs={{0,16},{16,0},{32,48},{48,32},{64,80},{80,64},{96,112},{112,96},{1... | collective-permute-start | bytes 1769480 | tf_op jit(solution)/shard_map/cond/branch_14_fun/ppermute | solution.py:175
  65.1 2.5 %collective-permute-start.98 = (f32[8,8]{1,0:T(8,128)S(1)}, f32[8,8]{1,0:T(8,128)S(1)}, u32[]{:S(2)}, u32[]{:S(2)}) collective-permute-start(f32[8,8]{1,0:T(8,128)S(1)} %get-tuple-element.31), channel_id=1, source_target_pairs={{0,1},{1,0},{2,3},{3,2},{4,5},{5,4},{6,7},{7,6},{8,9},{9,8},{10,11... | collective-permute-start | bytes 776 | tf_op jit(solution)/shard_map/ppermute | solution.py:191
  67.5 4.7 %collective-permute-start.99 = (f32[8,8]{1,0:T(8,128)S(1)}, f32[8,8]{1,0:T(8,128)S(1)}, u32[]{:S(2)}, u32[]{:S(2)}) collective-permute-start(f32[8,8]{1,0:T(8,128)S(1)} %add.204), channel_id=1, source_target_pairs={{0,3},{1,2},{2,1},{3,0},{4,7},{5,6},{6,5},{7,4},{8,11},{9,10},{10,... | collective-permute-start | bytes 776 | tf_op jit(solution)/shard_map/ppermute | solution.py:191
  72.2 15.6 %collective-permute-start.100 = (f32[8,8]{1,0:T(8,128)S(1)}, f32[8,8]{1,0:T(8,128)S(1)}, u32[]{:S(2)}, u32[]{:S(2)}) collective-permute-start(f32[8,8]{1,0:T(8,128)S(1)} %add.205), channel_id=1, source_target_pairs={{0,6},{1,7},{2,4},{3,5},{4,2},{5,3},{6,0},{7,1},{8,14},{9,15},{10,... | collective-permute-start | bytes 776 | tf_op jit(solution)/shard_map/ppermute | solution.py:191
  87.9 12.2 %collective-permute-start.101 = (f32[8,8]{1,0:T(8,128)S(1)}, f32[8,8]{1,0:T(8,128)S(1)}, u32[]{:S(2)}, u32[]{:S(2)}) collective-permute-start(f32[8,8]{1,0:T(8,128)S(1)} %add.206), channel_id=1, source_target_pairs={{0,8},{1,9},{2,10},{3,11},{4,12},{5,13},{6,14},{7,15},{8,0},{9,1},... | collective-permute-start | bytes 776 | tf_op jit(solution)/shard_map/ppermute | solution.py:191

commit v2 on v1

v2 whole, which is shorter than its diff:
```python
import itertools

import jax
import jax.numpy as jnp
from jax import lax
from jax.experimental import pallas as pl
from jax.experimental.pallas import tpu as pltpu
from jax.sharding import PartitionSpec as P

NY = 64
OWN = 8
LANES = 128
ROWS = 32
PAD = 2
DEPTH = 3
REACH = 3

C = 1.0 / 6.02


def weight(dx, dy, dz):
    steps = ((1, 0, 0), (-1, 0, 0), (0, 1, 0), (0, -1, 0), (0, 0, 1), (0, 0, -1))
    total = 0.0
    for length in range(REACH + 1):
        walks = sum(
            tuple(map(sum, zip((0, 0, 0), *walk))) == (dx, dy, dz)
            for walk in itertools.product(steps, repeat=length)
        )
        total += walks * C ** (length + 1)
    return total


WEIGHTS = {
    d: weight(*d)
    for d in itertools.product(range(REACH + 1), repeat=3)
    if sum(d) <= REACH
}


def spread_matrix():
    row = lax.broadcasted_iota(jnp.int32, (LANES, 2 * LANES), 0)
    col = lax.broadcasted_iota(jnp.int32, (LANES, 2 * LANES), 1)
    half = col // LANES
    lane = col % LANES
    source = (lane % 2 + half) % 2 * NY + lane // 2
    return jnp.where(row == source, 1.0, 0.0).astype(jnp.bfloat16)


def gather_matrix():
    row = lax.broadcasted_iota(jnp.int32, (LANES, LANES), 0)
    col = lax.broadcasted_iota(jnp.int32, (LANES, LANES), 1)
    source = col % NY * 2 + col // NY
    return jnp.where(row == source, 1.0, 0.0).astype(jnp.bfloat16)


def lay_out(source, spread):
    wide = source.astype(jnp.float32)
    count = wide.shape[1] // LANES
    tall = jnp.concatenate(
        [wide[:, r * LANES : (r + 1) * LANES] for r in range(count)], axis=0
    )
    both = jnp.dot(
        tall.astype(jnp.bfloat16), spread, preferred_element_type=jnp.float32
    )
    return both[:, :LANES], both[:, LANES:]


def finish_plane(even, swapped, even_ref, odd_ref, plane):
    lane = lax.broadcasted_iota(jnp.int32, (ROWS * OWN, LANES), 1)
    ahead = jnp.concatenate([swapped[OWN:], swapped[:OWN]], axis=0)
    odd = jnp.where(lane % 2 == 1, ahead, swapped)
    n, p = ROWS * OWN, PAD * OWN
    for ref, value in ((even_ref, even), (odd_ref, odd)):
        ref[plane, p : p + n] = value
        ref[plane, :p] = value[n - p :]
        ref[plane, p + n :] = value[:p]


def put_whole(source, spread, even_ref, odd_ref, plane):
    finish_plane(*lay_out(source, spread), even_ref, odd_ref, plane)


def put_halves(core, mine, other, spread, even_ref, odd_ref, plane):
    a, b = lay_out(mine, spread), lay_out(other, spread)
    first = [jnp.where(core == 0, s, t) for s, t in zip(a, b)]
    second = [jnp.where(core == 0, t, s) for s, t in zip(a, b)]
    both = [jnp.concatenate(pair, axis=0) for pair in zip(first, second)]
    finish_plane(*both, even_ref, odd_ref, plane)


def add_planes(pairs, phi, orb, acc_in, acc_out, here_plane):
    def tile_step(tile, carry):
        def read(field, z, dx, i):
            refs, plane = field(z)
            start = tile * (8 * OWN) + (PAD + dx // 2) * OWN + i
            return refs[dx % 2][plane, pl.ds(start, 8, stride=OWN), :]

        for z in range(DEPTH):
            if acc_in is None:
                total = [None] * OWN
            else:
                total = [
                    acc_in[z, pl.ds(tile * (8 * OWN) + j, 8, stride=OWN), :]
                    for j in range(OWN)
                ]
            centre = [read(here_plane, z, 0, i) for i in range(OWN)]
            for reach in range(REACH + 1):
                signs = (reach, -reach) if reach else (0,)
                here = [
                    [pltpu.roll(v, 2 * dy % LANES, 1) if dy else v for v in centre]
                    for dy in signs
                ]
                sums = [[None] * OWN for _ in signs]
                rest = REACH - reach
                for dz in range(-rest, rest + 1):
                    if (z, dz) not in pairs:
                        continue
                    for dx in range(abs(dz) - rest, rest - abs(dz) + 1):
                        g = [None for _ in signs]
                        for i in range(OWN):
                            there = read(phi, z + dz, dx, i)
                            for s in range(len(signs)):
                                term = here[s][i] * there
                                g[s] = term if g[s] is None else g[s] + term
                        scale = -WEIGHTS[abs(dx), reach, abs(dz)]
                        g = [v * scale for v in g]
                        for j in range(OWN):
                            there = read(orb, z + dz, dx, j)
                            for s in range(len(signs)):
                                term = g[s] * there
                                old = sums[s][j]
                                sums[s][j] = term if old is None else old + term
                for s, dy in enumerate(signs):
                    for j in range(OWN):
                        term = sums[s][j]
                        if term is None:
                            continue
                        if dy:
                            term = pltpu.roll(term, -2 * dy % LANES, 1)
                        total[j] = term if total[j] is None else total[j] + term
            for j in range(OWN):
                acc_out[z, pl.ds(tile * (8 * OWN) + j, 8, stride=OWN), :] = total[j]
        return carry

    lax.fori_loop(0, ROWS // 8, tile_step, 0)


INSIDE = [
    (z, dz)
    for z in range(DEPTH)
    for dz in range(-REACH, REACH + 1)
    if 0 <= z + dz < DEPTH
]
OUTSIDE = [
    (z, dz)
    for z in range(DEPTH)
    for dz in range(-REACH, REACH + 1)
    if not 0 <= z + dz < DEPTH
]


def inner_kernel(core, mine, other, own, acc, fa, fb, oa, ob):
    spread = spread_matrix()
    for z in range(DEPTH):
        put_halves(core[0], mine[z], other[z], spread, fa, fb, z)
        put_whole(own[z], spread, oa, ob, z)
    phi = lambda z: ((fa, fb), z)
    orb = lambda z: ((oa, ob), z)
    add_planes(INSIDE, phi, orb, None, acc, phi)


def outer_kernel(
    core, mine, other, far_mine, far_other, low, own, high, acc_in,
    out, part, here, fa, fb, oa, ob, acc,
):
    spread = spread_matrix()
    for z in range(DEPTH):
        a, b = lay_out(mine[z], spread)[0], lay_out(other[z], spread)[0]
        n = a.shape[0]
        here[z, PAD * OWN : PAD * OWN + n] = jnp.where(core[0] == 0, a, b)
        here[z, PAD * OWN + n : PAD * OWN + 2 * n] = jnp.where(core[0] == 0, b, a)
        put_whole(low[z], spread, oa, ob, z)
        put_whole(high[z], spread, oa, ob, DEPTH + z)
    for z in range(2 * DEPTH):
        put_halves(core[0], far_mine[z], far_other[z], spread, fa, fb, z)
    place = lambda z: z + DEPTH if z < 0 else z
    phi = lambda z: ((fa, fb), place(z))
    orb = lambda z: ((oa, ob), place(z))
    add_planes(OUTSIDE, phi, orb, acc_in, acc, lambda z: ((here,), z))

    gather = gather_matrix()
    products = None
    for z in range(DEPTH):
        tall = jnp.dot(
            acc[z].astype(jnp.bfloat16), gather, preferred_element_type=jnp.float32
        )
        wide = jnp.concatenate(
            [tall[r * OWN : (r + 1) * OWN] for r in range(ROWS)], axis=1
        ).astype(jnp.bfloat16)
        out[z] = wide
        term = lax.dot_general(
            own[z], wide, (((1,), (1,)), ((), ())), preferred_element_type=jnp.float32
        )
        products = term if products is None else products + term
    part[...] = products


def field(planes):
    return pltpu.VMEM((planes, (ROWS + 2 * PAD) * OWN, LANES), jnp.float32)


SUMS = (DEPTH, ROWS * OWN, LANES)
ON_CHIP = pl.BlockSpec(memory_space=pltpu.VMEM)
SCALAR = pl.BlockSpec(memory_space=pltpu.SMEM)
PARAMS = pltpu.CompilerParams(vmem_limit_bytes=32 * 1024 * 1024)


def inner(core, mine, other, own):
    return pl.pallas_call(
        inner_kernel,
        out_shape=jax.ShapeDtypeStruct(SUMS, jnp.float32),
        in_specs=[SCALAR] + [ON_CHIP] * 3,
        out_specs=ON_CHIP,
        scratch_shapes=[field(DEPTH)] * 4,
        compiler_params=PARAMS,
        cost_estimate=pl.CostEstimate(
            flops=40_000_000, bytes_accessed=1_000_000, transcendentals=0
        ),
    )(core, mine, other, own)


def outer(core, mine, other, far_mine, far_other, low, own, high, acc):
    return pl.pallas_call(
        outer_kernel,
        out_shape=(
            jax.ShapeDtypeStruct((DEPTH, OWN, ROWS * LANES), jnp.bfloat16),
            jax.ShapeDtypeStruct((OWN, OWN), jnp.float32),
        ),
        in_specs=[SCALAR] + [ON_CHIP] * 8,
        out_specs=[ON_CHIP] * 2,
        scratch_shapes=[field(DEPTH)]
        + [field(2 * DEPTH)] * 4
        + [pltpu.VMEM(SUMS, jnp.float32)],
        compiler_params=PARAMS,
        cost_estimate=pl.CostEstimate(
            flops=20_000_000, bytes_accessed=2_000_000, transcendentals=0
        ),
    )(core, mine, other, far_mine, far_other, low, own, high, acc)


def shift_pairs(count, step):
    return [(s, (s + step) % count) for s in range(count)]


def halo(x):
    count = lax.axis_size("dom")
    low = lax.ppermute(x, "dom", shift_pairs(count, 1))
    return low, lax.ppermute(x, "dom", shift_pairs(count, -1))


def swap(x, axis, bits):
    return lax.ppermute(x, axis, [(i, i ^ bits) for i in range(lax.axis_size(axis))])


def on_device(orbitals, block_owner):
    x = jnp.transpose(orbitals, (1, 0, 2))
    me = lax.axis_index("orb")
    core = me % 2
    half = x.shape[2] // 2
    cut = lambda v: lax.dynamic_slice_in_dim(v, core * half, half, 2)
    low, high = halo(x)
    from_mate = swap(x, "orb", 1)
    zero = jnp.zeros((), x.dtype)
    mine = jnp.where(me == block_owner[0], cut(x), zero)
    mine = jnp.where(me ^ 1 == block_owner[0], cut(from_mate), mine)
    for bits in (8, 2, 6):
        mine = mine + swap(mine, "orb", bits)
    low, high, mine = lax.optimization_barrier((low, high, mine))
    far = halo(mine)
    other = swap(mine, "orb", 1)
    index = core.reshape(1)
    acc = inner(index, mine, other, x)
    far_mine = jnp.concatenate(far, axis=0)
    far_other = swap(far_mine, "orb", 1)
    applied, total = outer(
        index, mine, other, far_mine, far_other, low, x, high, acc
    )
    for group in ((1, 2, 3), (6, 8, 14)):
        total = sum([swap(total, "dom", bits) for bits in group], total)
    return jnp.transpose(applied, (1, 0, 2)), total / 512.0


def solution(mesh):
    in_specs = (P("orb", "dom", None), P())
    out_specs = (P("orb", "dom", None), P("orb", None))
    return jax.shard_map(
        on_device, mesh=mesh, in_specs=in_specs, out_specs=out_specs, check_vma=False
    )
```

time: 98.9 us -> 66 us (0.67)
  the two profiles are of different devices: /device:TPU:1 before, /device:TPU:6 now
where the time goes in v2:
time: 66 us; the launch traced here: 65.9 us
  starting transfers between devices  31.5 us (48%)
  waiting for transfers between devices  22.9 us (35%)
  Pallas kernels  8.49 us (13%)
  other arithmetic  1.61 us (2%)
  between operations  1.39 us (2%)
    ppermute x12, starting transfers between devices, swap(): lax.ppermute(x, axis, [(i, i ^ bits) for i in range(lax.axis_size(axis))])  19.1 us
    ppermute x12, waiting for transfers between devices, swap(): lax.ppermute(x, axis, [(i, i ^ bits) for i in range(lax.axis_size(axis))])  17 us
    ppermute x2, starting transfers between devices, halo(): return (low, lax.ppermute(x, 'dom', shift_pairs(count, -1)))  12.3 us
    ppermute x2, waiting for transfers between devices, halo(): low = lax.ppermute(x, 'dom', shift_pairs(count, 1))  5.88 us
    pallas_call x1, Pallas kernels, inner(): pl.pallas_call(inner_kernel, out_shape=jax.ShapeDtypeStruct(SUMS, jnp.flo...  4.89 us
    pallas_call x1, Pallas kernels, outer(): pl.pallas_call(outer_kernel, out_shape=(jax.ShapeDtypeStruct((DEPTH, OWN,...  3.6 us
  transfers between devices with their start and end apart: 16, of which 10 were waited for; matrix products, arithmetic and copies ran while one was open for 0% of the time, Pallas kernels for 7%

profile of v2, /device:TPU:6, one launch (start us, length us, event | category | flops | bytes accessed | tf_op | source)
XLA Modules:
  0.0 65.9 jit_solution(11184037914933485639)
XLA Ops:
  0.6 0.1 collective-permute-start.2
  1.4 1.0 %collective-permute-done.2 = bf16[3,8,4096]{2,1,0:T(8,128)(2,1)S(1)} collective-permute-done((bf16[3,8,4096]{2,1,0:T(8,128)(2,1)}, bf16[3,8,4096]{2,1,0:T(8,128)(2,1)S(1)}, u32[]{:S(2)}, u32[]{:S(2)}) %collective-permute-start.2) | collective-permute-done | bytes 196640 | tf_op jit(solution)/shard_map/ppermute | solution.py:262
  2.4 0.9 %bitcast_select_fusion = bf16[3,8,2048]{2,1,0:T(8,128)(2,1)S(1)} fusion(bf16[8,3,4096]{2,0,1:T(8,128)(2,1)} %param.2, s32[]{:T(128)S(6)} %select_n.32, bf16[3,8,4096]{2,1,0:T(8,128)(2,1)S(1)} %collective-permute-done.2, pred[]{:T(512)S(6)} %eq.9, pred[]{:T(512)S(6)} %eq.8), kind=kLoop, calls=%fused_computation | loop fusion | flops 98304 | bytes 294918 | tf_op jit(solution)/shard_map/jit(_where)/select_n | solution.py:275
  3.3 0.0 copy-start
  3.3 0.9 %collective-permute-start.3 = (bf16[3,8,2048]{2,1,0:T(8,128)(2,1)S(1)}, bf16[3,8,2048]{2,1,0:T(8,128)(2,1)S(1)}, u32[]{:S(2)}, u32[]{:S(2)}) collective-permute-start(bf16[3,8,2048]{2,1,0:T(8,128)(2,1)S(1)} %bitcast_select_fusion), channel_id=1, source_target_pairs={{0,128},{16,144},{32,160},{48,176},{64,192},{80,208},{96,224},{112... | collective-permute-start | bytes 294920 | tf_op jit(solution)/shard_map/ppermute | solution.py:262
  4.2 4.0 %collective-permute-done.3 = bf16[3,8,2048]{2,1,0:T(8,128)(2,1)S(1)} collective-permute-done((bf16[3,8,2048]{2,1,0:T(8,128)(2,1)S(1)}, bf16[3,8,2048]{2,1,0:T(8,128)(2,1)S(1)}, u32[]{:S(2)}, u32[]{:S(2)}) %collective-permute-start.3) | collective-permute-done | bytes 98336 | tf_op jit(solution)/shard_map/ppermute | solution.py:262
  8.3 1.7 %collective-permute-start.4 = (bf16[3,8,2048]{2,1,0:T(8,128)(2,1)S(1)}, bf16[3,8,2048]{2,1,0:T(8,128)(2,1)S(1)}, u32[]{:S(2)}, u32[]{:S(2)}) collective-permute-start(bf16[3,8,2048]{2,1,0:T(8,128)(2,1)S(1)} %add.37), channel_id=1, source_target_pairs={{0,32},{16,48},{32,0},{48,16},{64,96},{80,112},{96,64},{112,80},{1... | collective-permute-start | bytes 294920 | tf_op jit(solution)/shard_map/ppermute | solution.py:262
  9.9 6.7 %collective-permute-start.1 = (bf16[3,8,4096]{2,1,0:T(8,128)(2,1)S(1)}, bf16[3,8,4096]{2,1,0:T(8,128)(2,1)S(1)}, u32[]{:S(2)}, u32[]{:S(2)}) collective-permute-start(bf16[3,8,4096]{2,1,0:T(8,128)(2,1)S(1)} %bitcast.9), channel_id=1, source_target_pairs={{0,15},{1,0},{2,1},{3,2},{4,3},{5,4},{6,5},{7,6},{8,7},{9,8},{10,9... | collective-permute-start | bytes 589832 | tf_op jit(solution)/shard_map/ppermute | solution.py:258
  16.6 0.0 collective-permute-done.4
  16.7 2.3 %collective-permute-start.5 = (bf16[3,8,2048]{2,1,0:T(8,128)(2,1)S(1)}, bf16[3,8,2048]{2,1,0:T(8,128)(2,1)S(1)}, u32[]{:S(2)}, u32[]{:S(2)}) collective-permute-start(bf16[3,8,2048]{2,1,0:T(8,128)(2,1)S(1)} %add.38), channel_id=1, source_target_pairs={{0,96},{16,112},{32,64},{48,80},{64,32},{80,48},{96,0},{112,16},{1... | collective-permute-start | bytes 294920 | tf_op jit(solution)/shard_map/ppermute | solution.py:262
  18.9 3.6 %collective-permute-done.5 = bf16[3,8,2048]{2,1,0:T(8,128)(2,1)S(1)} collective-permute-done((bf16[3,8,2048]{2,1,0:T(8,128)(2,1)S(1)}, bf16[3,8,2048]{2,1,0:T(8,128)(2,1)S(1)}, u32[]{:S(2)}, u32[]{:S(2)}) %collective-permute-start.5) | collective-permute-done | bytes 98336 | tf_op jit(solution)/shard_map/ppermute | solution.py:262
  22.6 0.0 collective-permute-done.1.high
  22.6 3.3 %collective-permute-done.low = bf16[3,8,4096]{2,1,0:T(8,128)(2,1)S(1)} collective-permute-done((bf16[3,8,4096]{2,1,0:T(8,128)(2,1)S(1)}, bf16[3,8,4096]{2,1,0:T(8,128)(2,1)S(1)}, u32[]{:S(2)}, u32[]{:S(2)}) %collective-permute-start) | collective-permute-done | bytes 196640 | tf_op jit(solution)/shard_map/ppermute | solution.py:257
  25.9 0.0 collective-permute-start.7
  25.9 5.6 %collective-permute-start.8 = (bf16[3,8,2048]{2,1,0:T(8,128)(2,1)S(1)}, bf16[3,8,2048]{2,1,0:T(8,128)(2,1)S(1)}, u32[]{:S(2)}, u32[]{:S(2)}) collective-permute-start(bf16[3,8,2048]{2,1,0:T(8,128)(2,1)S(1)} %add.39.mine), channel_id=1, source_target_pairs={{0,15},{1,0},{2,1},{3,2},{4,3},{5,4},{6,5},{7,6},{8,7},{9,8},{10,9... | collective-permute-start | bytes 294920 | tf_op jit(solution)/shard_map/ppermute | solution.py:258
  31.6 2.6 %collective-permute-done.7 = bf16[3,8,2048]{2,1,0:T(8,128)(2,1)S(1)} collective-permute-done((bf16[3,8,2048]{2,1,0:T(8,128)(2,1)S(1)}, bf16[3,8,2048]{2,1,0:T(8,128)(2,1)S(1)}, u32[]{:S(2)}, u32[]{:S(2)}) %collective-permute-start.7) | collective-permute-done | bytes 98336 | tf_op jit(solution)/shard_map/ppermute | solution.py:257
  34.2 0.0 collective-permute-done.8
  34.2 0.1 collective-permute-start.9
  34.3 0.5 collective-permute-start.6
  34.8 1.1 %collective-permute-done.6.other = bf16[3,8,2048]{2,1,0:T(8,128)(2,1)S(1)} collective-permute-done((bf16[3,8,2048]{2,1,0:T(8,128)(2,1)S(1)}, bf16[3,8,2048]{2,1,0:T(8,128)(2,1)S(1)}, u32[]{:S(2)}, u32[]{:S(2)}) %collective-permute-start.6) | collective-permute-done | bytes 98336 | tf_op jit(solution)/shard_map/ppermute | solution.py:262
  35.9 4.9 %shard_map.41.acc_in = f32[3,256,128]{2,1,0:T(8,128)S(1)} custom-call(s32[1]{0:T(128)} %bitcast.core, bf16[3,8,2048]{2,1,0:T(8,128)(2,1)S(1)} %add.39.mine, bf16[3,8,2048]{2,1,0:T(8,128)(2,1)S(1)} %collective-permute-done.6.other, bf16[3,8,4096]{2,1,0:T(8,128)(2,1)S(1)} %bitcast.11), custom_call_target="tpu_custom_call" | custom-call | flops 40000000 | bytes 1000000 | tf_op jit(solution)/shard_map/pallas_call | solution.py:219
  40.8 3.6 %shard_map.42 = (bf16[3,8,4096]{2,1,0:T(8,128)(2,1)}, f32[8,8]{1,0:T(8,128)S(1)}) custom-call(s32[1]{0:T(128)} %bitcast.core, bf16[3,8,2048]{2,1,0:T(8,128)(2,1)S(1)} %add.39.mine, bf16[3,8,2048]{2,1,0:T(8,128)(2,1)S(1)} %collective-permute-done.6.other, bf16[6,8,2048]{2,1,0:T(8,128)(2,1)S(1)} %constant_dynamic-update-slice_fusion.far_mine, ...), custom_call_target="tpu_custom_call" | custom-call | flops 20000000 | bytes 2000000 | tf_op jit(solution)/shard_map/pallas_call | solution.py:233
  44.4 0.0 collective-permute-start.12
  44.4 0.0 collective-permute-start.11
  44.4 4.4 %collective-permute-start.10 = (f32[8,8]{1,0:T(8,128)S(1)}, f32[8,8]{1,0:T(8,128)S(1)}, u32[]{:S(2)}, u32[]{:S(2)}) collective-permute-start(f32[8,8]{1,0:T(8,128)S(1)} %get-tuple-element.11), channel_id=1, source_target_pairs={{0,1},{1,0},{2,3},{3,2},{4,5},{5,4},{6,7},{7,6},{8,9},{9,8},{10,11... | collective-permute-start | bytes 776 | tf_op jit(solution)/shard_map/ppermute | solution.py:262
  48.8 1.0 %collective-permute-done.12 = f32[8,8]{1,0:T(8,128)S(1)} collective-permute-done((f32[8,8]{1,0:T(8,128)S(1)}, f32[8,8]{1,0:T(8,128)S(1)}, u32[]{:S(2)}, u32[]{:S(2)}) %collective-permute-start.12) | collective-permute-done | bytes 288 | tf_op jit(solution)/shard_map/ppermute | solution.py:262
  49.8 0.6 collective-permute-done.10
  50.3 7.1 %collective-permute-start.15 = (f32[8,8]{1,0:T(8,128)S(1)}, f32[8,8]{1,0:T(8,128)S(1)}, u32[]{:S(2)}, u32[]{:S(2)}) collective-permute-start(f32[8,8]{1,0:T(8,128)S(1)} %add_add_fusion), channel_id=1, source_target_pairs={{0,14},{1,15},{2,12},{3,13},{4,10},{5,11},{6,8},{7,9},{8,6},{9,7},... | collective-permute-start | bytes 776 | tf_op jit(solution)/shard_map/ppermute | solution.py:262
  57.4 2.1 %collective-permute-start.14 = (f32[8,8]{1,0:T(8,128)S(1)}, f32[8,8]{1,0:T(8,128)S(1)}, u32[]{:S(2)}, u32[]{:S(2)}) collective-permute-start(f32[8,8]{1,0:T(8,128)S(1)} %add_add_fusion), channel_id=1, source_target_pairs={{0,8},{1,9},{2,10},{3,11},{4,12},{5,13},{6,14},{7,15},{8,0},{9,1},... | collective-permute-start | bytes 776 | tf_op jit(solution)/shard_map/ppermute | solution.py:262
  59.5 3.0 %collective-permute-done.14 = f32[8,8]{1,0:T(8,128)S(1)} collective-permute-done((f32[8,8]{1,0:T(8,128)S(1)}, f32[8,8]{1,0:T(8,128)S(1)}, u32[]{:S(2)}, u32[]{:S(2)}) %collective-permute-start.14) | collective-permute-done | bytes 288 | tf_op jit(solution)/shard_map/ppermute | solution.py:262
  62.5 2.7 %collective-permute-done.13 = f32[8,8]{1,0:T(8,128)S(1)} collective-permute-done((f32[8,8]{1,0:T(8,128)S(1)}, f32[8,8]{1,0:T(8,128)S(1)}, u32[]{:S(2)}, u32[]{:S(2)}) %collective-permute-start.13) | collective-permute-done | bytes 288 | tf_op jit(solution)/shard_map/ppermute | solution.py:262
  65.3 0.6 add_multiply_fusion
  (12 shorter events, 0.1 us)
Async XLA Ops:
  0.6 1.7 %collective-permute-start.2 = (bf16[3,8,4096]{2,1,0:T(8,128)(2,1)}, bf16[3,8,4096]{2,1,0:T(8,128)(2,1)S(1)}, u32[]{:S(2)}, u32[]{:S(2)}) collective-permute-start(bf16[3,8,4096]{2,1,0:T(8,128)(2,1)} %bitcast.8), channel_id=1, source_target_pairs={{0,16},{16,0},{32,48},{48,32},{64,80},{80,64},{96,112},{112,96},{1... | collective-permute-start | bytes 589832 | tf_op jit(solution)/shard_map/ppermute | solution.py:262
  3.3 6.6 %copy-start = (bf16[8,3,4096]{2,0,1:T(8,128)(2,1)S(1)}, bf16[8,3,4096]{2,0,1:T(8,128)(2,1)}, u32[]{:S(2)}) copy-start(bf16[8,3,4096]{2,0,1:T(8,128)(2,1)} %param.2) | copy-start | bytes 589828
  3.3 4.9 %collective-permute-start.3 = (bf16[3,8,2048]{2,1,0:T(8,128)(2,1)S(1)}, bf16[3,8,2048]{2,1,0:T(8,128)(2,1)S(1)}, u32[]{:S(2)}, u32[]{:S(2)}) collective-permute-start(bf16[3,8,2048]{2,1,0:T(8,128)(2,1)S(1)} %bitcast_select_fusion), channel_id=1, source_target_pairs={{0,128},{16,144},{32,160},{48,176},{64,192},{80,208},{96,224},{112... | collective-permute-start | bytes 294920 | tf_op jit(solution)/shard_map/ppermute | solution.py:262
  8.3 8.4 %collective-permute-start.4 = (bf16[3,8,2048]{2,1,0:T(8,128)(2,1)S(1)}, bf16[3,8,2048]{2,1,0:T(8,128)(2,1)S(1)}, u32[]{:S(2)}, u32[]{:S(2)}) collective-permute-start(bf16[3,8,2048]{2,1,0:T(8,128)(2,1)S(1)} %add.37), channel_id=1, source_target_pairs={{0,32},{16,48},{32,0},{48,16},{64,96},{80,112},{96,64},{112,80},{1... | collective-permute-start | bytes 294920 | tf_op jit(solution)/shard_map/ppermute | solution.py:262
  9.9 12.7 %collective-permute-start.1 = (bf16[3,8,4096]{2,1,0:T(8,128)(2,1)S(1)}, bf16[3,8,4096]{2,1,0:T(8,128)(2,1)S(1)}, u32[]{:S(2)}, u32[]{:S(2)}) collective-permute-start(bf16[3,8,4096]{2,1,0:T(8,128)(2,1)S(1)} %bitcast.9), channel_id=1, source_target_pairs={{0,15},{1,0},{2,1},{3,2},{4,3},{5,4},{6,5},{7,6},{8,7},{9,8},{10,9... | collective-permute-start | bytes 589832 | tf_op jit(solution)/shard_map/ppermute | solution.py:258
  16.6 9.3 %collective-permute-start = (bf16[3,8,4096]{2,1,0:T(8,128)(2,1)S(1)}, bf16[3,8,4096]{2,1,0:T(8,128)(2,1)S(1)}, u32[]{:S(2)}, u32[]{:S(2)}) collective-permute-start(bf16[3,8,4096]{2,1,0:T(8,128)(2,1)S(1)} %bitcast.10), channel_id=1, source_target_pairs={{0,1},{1,2},{2,3},{3,4},{4,5},{5,6},{6,7},{7,8},{8,9},{9,10},{10,1... | collective-permute-start | bytes 589832 | tf_op jit(solution)/shard_map/ppermute | solution.py:257
  16.7 5.9 %collective-permute-start.5 = (bf16[3,8,2048]{2,1,0:T(8,128)(2,1)S(1)}, bf16[3,8,2048]{2,1,0:T(8,128)(2,1)S(1)}, u32[]{:S(2)}, u32[]{:S(2)}) collective-permute-start(bf16[3,8,2048]{2,1,0:T(8,128)(2,1)S(1)} %add.38), channel_id=1, source_target_pairs={{0,96},{16,112},{32,64},{48,80},{64,32},{80,48},{96,0},{112,16},{1... | collective-permute-start | bytes 294920 | tf_op jit(solution)/shard_map/ppermute | solution.py:262
  25.9 8.2 %collective-permute-start.7 = (bf16[3,8,2048]{2,1,0:T(8,128)(2,1)S(1)}, bf16[3,8,2048]{2,1,0:T(8,128)(2,1)S(1)}, u32[]{:S(2)}, u32[]{:S(2)}) collective-permute-start(bf16[3,8,2048]{2,1,0:T(8,128)(2,1)S(1)} %add.39.mine), channel_id=1, source_target_pairs={{0,1},{1,2},{2,3},{3,4},{4,5},{5,6},{6,7},{7,8},{8,9},{9,10},{10,1... | collective-permute-start | bytes 294920 | tf_op jit(solution)/shard_map/ppermute | solution.py:257
  25.9 8.2 %collective-permute-start.8 = (bf16[3,8,2048]{2,1,0:T(8,128)(2,1)S(1)}, bf16[3,8,2048]{2,1,0:T(8,128)(2,1)S(1)}, u32[]{:S(2)}, u32[]{:S(2)}) collective-permute-start(bf16[3,8,2048]{2,1,0:T(8,128)(2,1)S(1)} %add.39.mine), channel_id=1, source_target_pairs={{0,15},{1,0},{2,1},{3,2},{4,3},{5,4},{6,5},{7,6},{8,7},{9,8},{10,9... | collective-permute-start | bytes 294920 | tf_op jit(solution)/shard_map/ppermute | solution.py:258
  34.2 6.6 %collective-permute-start.9 = (bf16[6,8,2048]{2,1,0:T(8,128)(2,1)S(1)}, bf16[6,8,2048]{2,1,0:T(8,128)(2,1)S(1)}, u32[]{:S(2)}, u32[]{:S(2)}) collective-permute-start(bf16[6,8,2048]{2,1,0:T(8,128)(2,1)S(1)} %constant_dynamic-update-slice_fusion.far_mine), channel_id=1, source_target_pairs={{0,16},{16,0},{32,48},{48,32},{64,80},{80,64},{96,112},{112,96},{1... | collective-permute-start | bytes 589832 | tf_op jit(solution)/shard_map/ppermute | solution.py:262
  34.3 1.6 %collective-permute-start.6 = (bf16[3,8,2048]{2,1,0:T(8,128)(2,1)S(1)}, bf16[3,8,2048]{2,1,0:T(8,128)(2,1)S(1)}, u32[]{:S(2)}, u32[]{:S(2)}) collective-permute-start(bf16[3,8,2048]{2,1,0:T(8,128)(2,1)S(1)} %add.39.mine), channel_id=1, source_target_pairs={{0,16},{16,0},{32,48},{48,32},{64,80},{80,64},{96,112},{112,96},{1... | collective-permute-start | bytes 294920 | tf_op jit(solution)/shard_map/ppermute | solution.py:262
  44.4 5.4 %collective-permute-start.12 = (f32[8,8]{1,0:T(8,128)S(1)}, f32[8,8]{1,0:T(8,128)S(1)}, u32[]{:S(2)}, u32[]{:S(2)}) collective-permute-start(f32[8,8]{1,0:T(8,128)S(1)} %get-tuple-element.11), channel_id=1, source_target_pairs={{0,3},{1,2},{2,1},{3,0},{4,7},{5,6},{6,5},{7,4},{8,11},{9,10},{10,... | collective-permute-start | bytes 776 | tf_op jit(solution)/shard_map/ppermute | solution.py:262
  44.4 5.4 %collective-permute-start.11 = (f32[8,8]{1,0:T(8,128)S(1)}, f32[8,8]{1,0:T(8,128)S(1)}, u32[]{:S(2)}, u32[]{:S(2)}) collective-permute-start(f32[8,8]{1,0:T(8,128)S(1)} %get-tuple-element.11), channel_id=1, source_target_pairs={{0,2},{1,3},{2,0},{3,1},{4,6},{5,7},{6,4},{7,5},{8,10},{9,11},{10,... | collective-permute-start | bytes 776 | tf_op jit(solution)/shard_map/ppermute | solution.py:262
  44.4 6.0 %collective-permute-start.10 = (f32[8,8]{1,0:T(8,128)S(1)}, f32[8,8]{1,0:T(8,128)S(1)}, u32[]{:S(2)}, u32[]{:S(2)}) collective-permute-start(f32[8,8]{1,0:T(8,128)S(1)} %get-tuple-element.11), channel_id=1, source_target_pairs={{0,1},{1,0},{2,3},{3,2},{4,5},{5,4},{6,7},{7,6},{8,9},{9,8},{10,11... | collective-permute-start | bytes 776 | tf_op jit(solution)/shard_map/ppermute | solution.py:262
  50.3 9.2 %collective-permute-start.15 = (f32[8,8]{1,0:T(8,128)S(1)}, f32[8,8]{1,0:T(8,128)S(1)}, u32[]{:S(2)}, u32[]{:S(2)}) collective-permute-start(f32[8,8]{1,0:T(8,128)S(1)} %add_add_fusion), channel_id=1, source_target_pairs={{0,14},{1,15},{2,12},{3,13},{4,10},{5,11},{6,8},{7,9},{8,6},{9,7},... | collective-permute-start | bytes 776 | tf_op jit(solution)/shard_map/ppermute | solution.py:262
  57.4 5.1 %collective-permute-start.14 = (f32[8,8]{1,0:T(8,128)S(1)}, f32[8,8]{1,0:T(8,128)S(1)}, u32[]{:S(2)}, u32[]{:S(2)}) collective-permute-start(f32[8,8]{1,0:T(8,128)S(1)} %add_add_fusion), channel_id=1, source_target_pairs={{0,8},{1,9},{2,10},{3,11},{4,12},{5,13},{6,14},{7,15},{8,0},{9,1},... | collective-permute-start | bytes 776 | tf_op jit(solution)/shard_map/ppermute | solution.py:262
  59.5 5.7 %collective-permute-start.13 = (f32[8,8]{1,0:T(8,128)S(1)}, f32[8,8]{1,0:T(8,128)S(1)}, u32[]{:S(2)}, u32[]{:S(2)}) collective-permute-start(f32[8,8]{1,0:T(8,128)S(1)} %add_add_fusion), channel_id=1, source_target_pairs={{0,6},{1,7},{2,4},{3,5},{4,2},{5,3},{6,0},{7,1},{8,14},{9,15},{10,... | collective-permute-start | bytes 776 | tf_op jit(solution)/shard_map/ppermute | solution.py:262

commit v3 on v2

--- a/solution.py
+++ b/solution.py
@@ -10,6 +10,7 @@
 NY = 64
 OWN = 8
 LANES = 128
+CELLS = 4096
 ROWS = 32
 PAD = 2
 DEPTH = 3
@@ -80,12 +81,10 @@
     finish_plane(*lay_out(source, spread), even_ref, odd_ref, plane)
 
 
-def put_halves(core, mine, other, spread, even_ref, odd_ref, plane):
-    a, b = lay_out(mine, spread), lay_out(other, spread)
-    first = [jnp.where(core == 0, s, t) for s, t in zip(a, b)]
-    second = [jnp.where(core == 0, t, s) for s, t in zip(a, b)]
-    both = [jnp.concatenate(pair, axis=0) for pair in zip(first, second)]
-    finish_plane(*both, even_ref, odd_ref, plane)
+def whole(core, mine, other):
+    return jnp.concatenate(
+        [jnp.where(core == 0, mine, other), jnp.where(core == 0, other, mine)], axis=1
+    )
 
 
 def add_planes(pairs, phi, orb, acc_in, acc_out, here_plane):
@@ -159,10 +158,15 @@
 ]
 
 
-def inner_kernel(core, mine, other, own, acc, fa, fb, oa, ob):
+def kind_of(index):
+    return (index ^ (index >> 1) ^ (index >> 3)) & 1
+
+
+def inner_kernel(mine, other, own, acc, fa, fb, oa, ob):
     spread = spread_matrix()
+    kind = kind_of(lax.axis_index("orb"))
     for z in range(DEPTH):
-        put_halves(core[0], mine[z], other[z], spread, fa, fb, z)
+        put_whole(whole(kind, mine[z], other[z]), spread, fa, fb, z)
         put_whole(own[z], spread, oa, ob, z)
     phi = lambda z: ((fa, fb), z)
     orb = lambda z: ((oa, ob), z)
@@ -170,22 +174,27 @@
 
 
 def outer_kernel(
-    core, mine, other, far_mine, far_other, low, own, high, acc_in,
+    mine, other, first, second, first_mine, second_mine, first_other, second_other,
+    own, acc_in,
     out, part, here, fa, fb, oa, ob, acc,
 ):
     spread = spread_matrix()
+    core = kind_of(lax.axis_index("orb"))
+    base = first_is_above(lax.axis_index("orb"), lax.axis_index("dom")) * DEPTH
+    rest = DEPTH - base
     for z in range(DEPTH):
-        a, b = lay_out(mine[z], spread)[0], lay_out(other[z], spread)[0]
-        n = a.shape[0]
-        here[z, PAD * OWN : PAD * OWN + n] = jnp.where(core[0] == 0, a, b)
-        here[z, PAD * OWN + n : PAD * OWN + 2 * n] = jnp.where(core[0] == 0, b, a)
-        put_whole(low[z], spread, oa, ob, z)
-        put_whole(high[z], spread, oa, ob, DEPTH + z)
-    for z in range(2 * DEPTH):
-        put_halves(core[0], far_mine[z], far_other[z], spread, fa, fb, z)
-    place = lambda z: z + DEPTH if z < 0 else z
-    phi = lambda z: ((fa, fb), place(z))
-    orb = lambda z: ((oa, ob), place(z))
+        centre = lay_out(whole(core, mine[z], other[z]), spread)[0]
+        here[z, PAD * OWN : (PAD + ROWS) * OWN] = centre
+        for orbs, halves, plane in (
+            (first, (first_mine, first_other), base + z),
+            (second, (second_mine, second_other), rest + z),
+        ):
+            phis = whole(core, halves[0][z], halves[1][z])
+            put_whole(orbs[z], spread, oa, ob, plane)
+            put_whole(phis, spread, fa, fb, plane)
+    plane_of = lambda z: z + DEPTH if z < 0 else z
+    phi = lambda z: ((fa, fb), plane_of(z))
+    orb = lambda z: ((oa, ob), plane_of(z))
     add_planes(OUTSIDE, phi, orb, acc_in, acc, lambda z: ((here,), z))
 
     gather = gather_matrix()
@@ -211,32 +220,31 @@
 
 SUMS = (DEPTH, ROWS * OWN, LANES)
 ON_CHIP = pl.BlockSpec(memory_space=pltpu.VMEM)
-SCALAR = pl.BlockSpec(memory_space=pltpu.SMEM)
 PARAMS = pltpu.CompilerParams(vmem_limit_bytes=32 * 1024 * 1024)
 
 
-def inner(core, mine, other, own):
+def inner(mine, other, own):
     return pl.pallas_call(
         inner_kernel,
         out_shape=jax.ShapeDtypeStruct(SUMS, jnp.float32),
-        in_specs=[SCALAR] + [ON_CHIP] * 3,
+        in_specs=[ON_CHIP] * 3,
         out_specs=ON_CHIP,
         scratch_shapes=[field(DEPTH)] * 4,
         compiler_params=PARAMS,
         cost_estimate=pl.CostEstimate(
             flops=40_000_000, bytes_accessed=1_000_000, transcendentals=0
         ),
-    )(core, mine, other, own)
-
-
-def outer(core, mine, other, far_mine, far_other, low, own, high, acc):
+    )(mine, other, own)
+
+
+def outer(*parts):
     return pl.pallas_call(
         outer_kernel,
         out_shape=(
             jax.ShapeDtypeStruct((DEPTH, OWN, ROWS * LANES), jnp.bfloat16),
             jax.ShapeDtypeStruct((OWN, OWN), jnp.float32),
         ),
-        in_specs=[SCALAR] + [ON_CHIP] * 8,
+        in_specs=[ON_CHIP] * 10,
         out_specs=[ON_CHIP] * 2,
         scratch_shapes=[field(DEPTH)]
         + [field(2 * DEPTH)] * 4
@@ -245,48 +253,58 @@
         cost_estimate=pl.CostEstimate(
             flops=20_000_000, bytes_accessed=2_000_000, transcendentals=0
         ),
-    )(core, mine, other, far_mine, far_other, low, own, high, acc)
-
-
-def shift_pairs(count, step):
-    return [(s, (s + step) % count) for s in range(count)]
-
-
-def halo(x):
-    count = lax.axis_size("dom")
-    low = lax.ppermute(x, "dom", shift_pairs(count, 1))
-    return low, lax.ppermute(x, "dom", shift_pairs(count, -1))
-
-
-def swap(x, axis, bits):
-    return lax.ppermute(x, axis, [(i, i ^ bits) for i in range(lax.axis_size(axis))])
+    )(*parts)
+
+
+def swap(x, axis, bits_of):
+    size = lax.axis_size(axis)
+    return lax.ppermute(x, axis, [(i, i ^ bits_of(i)) for i in range(size)])
+
+
+def first_is_above(orb, dom):
+    return (dom + (orb >> 3)) & 1
+
+
+def swap_slabs(x):
+    axes = ("orb", "dom")
+    groups, count = map(lax.axis_size, axes)
+
+    def swap_one(first):
+        pairs = []
+        for g, s in itertools.product(range(groups), range(count)):
+            up = first_is_above(g, s) == first
+            target = (s + (1 if up else -1)) % count
+            pairs.append((g * count + s, g * count + target))
+        return lax.ppermute(x, axes, pairs)
+
+    return swap_one(True), swap_one(False)
 
 
 def on_device(orbitals, block_owner):
     x = jnp.transpose(orbitals, (1, 0, 2))
     me = lax.axis_index("orb")
-    core = me % 2
+    owner = block_owner[0]
+    kind = kind_of(me)
     half = x.shape[2] // 2
-    cut = lambda v: lax.dynamic_slice_in_dim(v, core * half, half, 2)
-    low, high = halo(x)
-    from_mate = swap(x, "orb", 1)
-    zero = jnp.zeros((), x.dtype)
-    mine = jnp.where(me == block_owner[0], cut(x), zero)
-    mine = jnp.where(me ^ 1 == block_owner[0], cut(from_mate), mine)
-    for bits in (8, 2, 6):
-        mine = mine + swap(mine, "orb", bits)
-    low, high, mine = lax.optimization_barrier((low, high, mine))
-    far = halo(mine)
-    other = swap(mine, "orb", 1)
-    index = core.reshape(1)
-    acc = inner(index, mine, other, x)
-    far_mine = jnp.concatenate(far, axis=0)
-    far_other = swap(far_mine, "orb", 1)
-    applied, total = outer(
-        index, mine, other, far_mine, far_other, low, x, high, acc
-    )
-    for group in ((1, 2, 3), (6, 8, 14)):
-        total = sum([swap(total, "dom", bits) for bits in group], total)
+    cut = lambda v: jnp.where(kind == 0, v[:, :, :half], v[:, :, half:])
+    first, second = swap_slabs(x)
+    from_mate = swap(x, "orb", lambda i: 1)
+    mine = jnp.where(me == owner, cut(x), cut(from_mate))
+    known = 1
+    for by_kind in ((8, 2), (2, 6), (6, 8)):
+        theirs = swap(mine, "orb", lambda i: by_kind[kind_of(i)] ^ 1)
+        have = (me ^ owner) & ~known == 0
+        mine = jnp.where(have, mine, theirs)
+        known = known | jnp.where(kind == 0, by_kind[0], by_kind[1])
+    far = swap_slabs(mine)
+    other = swap(mine, "orb", lambda i: 1)
+    acc = inner(mine, other, x)
+    *far, acc, first, second = lax.optimization_barrier((*far, acc, first, second))
+    others = [swap(v, "orb", lambda i: 1) for v in far]
+    applied, total = outer(mine, other, first, second, *far, *others, x, acc)
+    total = lax.all_to_all(
+        jnp.broadcast_to(total[None], (lax.axis_size("dom"), OWN, OWN)), "dom", 0, 0
+    ).sum(0)
     return jnp.transpose(applied, (1, 0, 2)), total / 512.0
 
 

time: 66 us -> 52.7 us (0.80)
  the two profiles are of different devices: /device:TPU:6 before, /device:TPU:1 now
where the time goes in v3:
time: 52.7 us; the launch traced here: 52.6 us
  starting transfers between devices  17.5 us (33%)
  blocking collectives  12.5 us (24%)
  waiting for transfers between devices  11.1 us (21%)
  Pallas kernels  8.46 us (16%)
  other arithmetic  1.62 us (3%)
  between operations  1.38 us (3%)
    all_to_all x1, blocking collectives, on_device(): lax.all_to_all(jnp.broadcast_to(total[None], (lax.axis_size('dom'), OWN,...  12.5 us
    ppermute x7, waiting for transfers between devices, swap(): return lax.ppermute(x, axis, [(i, i ^ bits_of(i)) for i in range(size)])  9.95 us
    ppermute x4, starting transfers between devices, swap_one(): return lax.ppermute(x, axes, pairs)  9.92 us
    ppermute x7, starting transfers between devices, swap(): return lax.ppermute(x, axis, [(i, i ^ bits_of(i)) for i in range(size)])  7.55 us
    pallas_call x1, Pallas kernels, inner(): pl.pallas_call(inner_kernel, out_shape=jax.ShapeDtypeStruct(SUMS, jnp.flo...  4.88 us
    pallas_call x1, Pallas kernels, outer(): pl.pallas_call(outer_kernel, out_shape=(jax.ShapeDtypeStruct((DEPTH, OWN,...  3.57 us
    ppermute x4, waiting for transfers between devices, swap_one(): return lax.ppermute(x, axes, pairs)  1.16 us
  transfers between devices with their start and end apart: 11, of which 6 were waited for; matrix products, arithmetic and copies ran while one was open for 0% of the time, Pallas kernels for 9%

profile of v3, /device:TPU:1, one launch (start us, length us, event | category | flops | bytes accessed | tf_op | source)
XLA Modules:
  0.0 52.6 jit_solution(16025193142169386295)
XLA Ops:
  0.6 3.3 %collective-permute-start = (bf16[3,8,4096]{2,1,0:T(8,128)(2,1)}, bf16[3,8,4096]{2,1,0:T(8,128)(2,1)S(1)}, u32[]{:S(2)}, u32[]{:S(2)}) collective-permute-start(bf16[3,8,4096]{2,1,0:T(8,128)(2,1)} %bitcast.5), channel_id=1, source_target_pairs={{0,16},{16,0},{32,48},{48,32},{64,80},{80,64},{96,112},{112,96},{1... | collective-permute-start | bytes 589832 | tf_op jit(solution)/shard_map/ppermute | solution.py:261
  4.6 0.6 %collective-permute-done = bf16[3,8,4096]{2,1,0:T(8,128)(2,1)S(1)} collective-permute-done((bf16[3,8,4096]{2,1,0:T(8,128)(2,1)}, bf16[3,8,4096]{2,1,0:T(8,128)(2,1)S(1)}, u32[]{:S(2)}, u32[]{:S(2)}) %collective-permute-start) | collective-permute-done | bytes 196640 | tf_op jit(solution)/shard_map/ppermute | solution.py:261
  5.2 1.0 %fusion = bf16[3,8,2048]{2,1,0:T(8,128)(2,1)S(1)} fusion(bf16[3,8,4096]{2,1,0:T(8,128)(2,1)S(1)} %collective-permute-done, bf16[3,8,4096]{2,1,0:T(8,128)(2,1)} %bitcast.6, pred[]{:T(512)S(6)} %eq.18, pred[]{:T(512)S(6)} %eq.22), kind=kLoop, calls=%fused_computation.1 | loop fusion | flops 147456 | bytes 491522 | tf_op jit(solution)/shard_map/jit(_where)/select_n | solution.py:292
  6.2 0.1 collective-permute-start.1
  6.3 4.0 %collective-permute-done.1 = bf16[3,8,2048]{2,1,0:T(8,128)(2,1)S(1)} collective-permute-done((bf16[3,8,2048]{2,1,0:T(8,128)(2,1)S(1)}, bf16[3,8,2048]{2,1,0:T(8,128)(2,1)S(1)}, u32[]{:S(2)}, u32[]{:S(2)}) %collective-permute-start.1) | collective-permute-done | bytes 98336 | tf_op jit(solution)/shard_map/ppermute | solution.py:261
  10.3 0.0 copy-start
  10.4 1.3 %collective-permute-start.2 = (bf16[3,8,2048]{2,1,0:T(8,128)(2,1)S(1)}, bf16[3,8,2048]{2,1,0:T(8,128)(2,1)S(1)}, u32[]{:S(2)}, u32[]{:S(2)}) collective-permute-start(bf16[3,8,2048]{2,1,0:T(8,128)(2,1)S(1)} %broadcast_select_fusion), channel_id=1, source_target_pairs={{0,48},{16,96},{32,80},{48,0},{64,112},{80,32},{96,16},{112,64},{1... | collective-permute-start | bytes 294920 | tf_op jit(solution)/shard_map/ppermute | solution.py:261
  11.7 4.0 %collective-permute-done.2 = bf16[3,8,2048]{2,1,0:T(8,128)(2,1)S(1)} collective-permute-done((bf16[3,8,2048]{2,1,0:T(8,128)(2,1)S(1)}, bf16[3,8,2048]{2,1,0:T(8,128)(2,1)S(1)}, u32[]{:S(2)}, u32[]{:S(2)}) %collective-permute-start.2) | collective-permute-done | bytes 98336 | tf_op jit(solution)/shard_map/ppermute | solution.py:261
  15.7 0.1 collective-permute-start.3
  15.8 0.0 copy-done
  15.8 1.3 %collective-permute-start.8 = (bf16[3,8,4096]{2,1,0:T(8,128)(2,1)S(1)}, bf16[3,8,4096]{2,1,0:T(8,128)(2,1)S(1)}, u32[]{:S(2)}, u32[]{:S(2)}) collective-permute-start(bf16[3,8,4096]{2,1,0:T(8,128)(2,1)S(1)} %bitcast.7), channel_id=1, source_target_pairs={{0,1},{1,0},{2,3},{3,2},{4,5},{5,4},{6,7},{7,6},{8,9},{9,8},{10,11... | collective-permute-start | bytes 589832 | tf_op jit(solution)/shard_map/ppermute | solution.py:278
  17.2 6.8 %collective-permute-start.7 = (bf16[3,8,4096]{2,1,0:T(8,128)(2,1)S(1)}, bf16[3,8,4096]{2,1,0:T(8,128)(2,1)S(1)}, u32[]{:S(2)}, u32[]{:S(2)}) collective-permute-start(bf16[3,8,4096]{2,1,0:T(8,128)(2,1)S(1)} %bitcast.8), channel_id=1, source_target_pairs={{0,15},{1,2},{2,1},{3,4},{4,3},{5,6},{6,5},{7,8},{8,7},{9,10},{10,... | collective-permute-start | bytes 589832 | tf_op jit(solution)/shard_map/ppermute | solution.py:278
  24.0 0.0 collective-permute-done.3
  24.0 1.7 %collective-permute-start.4 = (bf16[3,8,2048]{2,1,0:T(8,128)(2,1)S(1)}, bf16[3,8,2048]{2,1,0:T(8,128)(2,1)S(1)}, u32[]{:S(2)}, u32[]{:S(2)}) collective-permute-start(bf16[3,8,2048]{2,1,0:T(8,128)(2,1)S(1)} %broadcast_select_fusion.2.mine), channel_id=1, source_target_pairs={{0,16},{16,0},{32,48},{48,32},{64,80},{80,64},{96,112},{112,96},{1... | collective-permute-start | bytes 294920 | tf_op jit(solution)/shard_map/ppermute | solution.py:261
  25.7 0.0 collective-permute-start.6
  25.7 1.7 %collective-permute-start.5 = (bf16[3,8,2048]{2,1,0:T(8,128)(2,1)S(1)}, bf16[3,8,2048]{2,1,0:T(8,128)(2,1)S(1)}, u32[]{:S(2)}, u32[]{:S(2)}) collective-permute-start(bf16[3,8,2048]{2,1,0:T(8,128)(2,1)S(1)} %broadcast_select_fusion.2.mine), channel_id=1, source_target_pairs={{0,15},{1,2},{2,1},{3,4},{4,3},{5,6},{6,5},{7,8},{8,7},{9,10},{10,... | collective-permute-start | bytes 294920 | tf_op jit(solution)/shard_map/ppermute | solution.py:278
  27.5 0.0 collective-permute-done.4.other
  27.5 4.9 %shard_map.41.acc_in = f32[3,256,128]{2,1,0:T(8,128)S(1)} custom-call(bf16[3,8,2048]{2,1,0:T(8,128)(2,1)S(1)} %broadcast_select_fusion.2.mine, bf16[3,8,2048]{2,1,0:T(8,128)(2,1)S(1)} %collective-permute-done.4.other, bf16[3,8,4096]{2,1,0:T(8,128)(2,1)S(1)} %bitcast.9), custom_call_target="tpu_custom_call" | custom-call | flops 40000000 | bytes 1000000 | tf_op jit(solution)/shard_map/pallas_call | solution.py:227
  32.3 0.0 collective-permute-done.8.second
  32.4 0.0 collective-permute-done.7.first
  32.4 0.0 collective-permute-done.6.second_mine
  32.4 1.2 %collective-permute-done.5.first_mine = bf16[3,8,2048]{2,1,0:T(8,128)(2,1)S(1)} collective-permute-done((bf16[3,8,2048]{2,1,0:T(8,128)(2,1)S(1)}, bf16[3,8,2048]{2,1,0:T(8,128)(2,1)S(1)}, u32[]{:S(2)}, u32[]{:S(2)}) %collective-permute-start.5) | collective-permute-done | bytes 98336 | tf_op jit(solution)/shard_map/ppermute | solution.py:278
  33.5 1.0 %collective-permute-start.9 = (bf16[3,8,2048]{2,1,0:T(8,128)(2,1)S(1)}, bf16[3,8,2048]{2,1,0:T(8,128)(2,1)S(1)}, u32[]{:S(2)}, u32[]{:S(2)}) collective-permute-start(bf16[3,8,2048]{2,1,0:T(8,128)(2,1)S(1)} %collective-permute-done.5.first_mine), channel_id=1, source_target_pairs={{0,16},{16,0},{32,48},{48,32},{64,80},{80,64},{96,112},{112,96},{1... | collective-permute-start | bytes 294920 | tf_op jit(solution)/shard_map/ppermute | solution.py:261
  34.5 0.0 collective-permute-start.10
  34.5 0.9 %collective-permute-done.9.first_other = bf16[3,8,2048]{2,1,0:T(8,128)(2,1)S(1)} collective-permute-done((bf16[3,8,2048]{2,1,0:T(8,128)(2,1)S(1)}, bf16[3,8,2048]{2,1,0:T(8,128)(2,1)S(1)}, u32[]{:S(2)}, u32[]{:S(2)}) %collective-permute-start.9) | collective-permute-done | bytes 98336 | tf_op jit(solution)/shard_map/ppermute | solution.py:261
  35.5 0.4 collective-permute-done.10.second_other
  35.8 3.6 %shard_map.42 = (bf16[3,8,4096]{2,1,0:T(8,128)(2,1)}, f32[8,8]{1,0:T(8,128)S(1)}) custom-call(bf16[3,8,2048]{2,1,0:T(8,128)(2,1)S(1)} %broadcast_select_fusion.2.mine, bf16[3,8,2048]{2,1,0:T(8,128)(2,1)S(1)} %collective-permute-done.4.other, bf16[3,8,4096]{2,1,0:T(8,128)(2,1)S(1)} %collective-permute-done.7.first, ...), custom_call_target="tpu_custom_call" | custom-call | flops 20000000 | bytes 2000000 | tf_op jit(solution)/shard_map/pallas_call | solution.py:241
  39.4 12.5 %all_to_all.5 = f32[16,8,8]{2,1,0:T(8,128)S(1)} all-to-all(f32[16,8,8]{2,1,0:T(8,128)S(1)} %broadcast_in_dim.2), channel_id=1, replica_groups=mesh['orb'=16,'dom'=16] {'dom'}, dimensions={0} | all-to-all | bytes 8192 | tf_op jit(solution)/shard_map/all_to_all | solution.py:305
  52.0 0.6 %broadcast_multiply_fusion = f32[8,8]{1,0:T(8,128)} fusion(f32[8,8]{1,0:T(8,128)S(1)} %reduce_sum.9), kind=kLoop, calls=%fused_computation.6 | loop fusion | flops 64 | bytes 512 | tf_op jit(solution)/shard_map/div | solution.py:308
  (5 shorter events, 0.1 us)
Async XLA Ops:
  0.6 4.6 %collective-permute-start = (bf16[3,8,4096]{2,1,0:T(8,128)(2,1)}, bf16[3,8,4096]{2,1,0:T(8,128)(2,1)S(1)}, u32[]{:S(2)}, u32[]{:S(2)}) collective-permute-start(bf16[3,8,4096]{2,1,0:T(8,128)(2,1)} %bitcast.5), channel_id=1, source_target_pairs={{0,16},{16,0},{32,48},{48,32},{64,80},{80,64},{96,112},{112,96},{1... | collective-permute-start | bytes 589832 | tf_op jit(solution)/shard_map/ppermute | solution.py:261
  6.2 4.1 %collective-permute-start.1 = (bf16[3,8,2048]{2,1,0:T(8,128)(2,1)S(1)}, bf16[3,8,2048]{2,1,0:T(8,128)(2,1)S(1)}, u32[]{:S(2)}, u32[]{:S(2)}) collective-permute-start(bf16[3,8,2048]{2,1,0:T(8,128)(2,1)S(1)} %fusion), channel_id=1, source_target_pairs={{0,144},{16,32},{32,16},{48,160},{64,208},{80,96},{96,80},{112,224... | collective-permute-start | bytes 294920 | tf_op jit(solution)/shard_map/ppermute | solution.py:261
  10.3 5.5 %copy-start = (bf16[8,3,4096]{2,0,1:T(8,128)(2,1)S(1)}, bf16[8,3,4096]{2,0,1:T(8,128)(2,1)}, u32[]{:S(2)}) copy-start(bf16[8,3,4096]{2,0,1:T(8,128)(2,1)} %param.2) | copy-start | bytes 589828
  10.4 5.3 %collective-permute-start.2 = (bf16[3,8,2048]{2,1,0:T(8,128)(2,1)S(1)}, bf16[3,8,2048]{2,1,0:T(8,128)(2,1)S(1)}, u32[]{:S(2)}, u32[]{:S(2)}) collective-permute-start(bf16[3,8,2048]{2,1,0:T(8,128)(2,1)S(1)} %broadcast_select_fusion), channel_id=1, source_target_pairs={{0,48},{16,96},{32,80},{48,0},{64,112},{80,32},{96,16},{112,64},{1... | collective-permute-start | bytes 294920 | tf_op jit(solution)/shard_map/ppermute | solution.py:261
  15.7 8.3 %collective-permute-start.3 = (bf16[3,8,2048]{2,1,0:T(8,128)(2,1)S(1)}, bf16[3,8,2048]{2,1,0:T(8,128)(2,1)S(1)}, u32[]{:S(2)}, u32[]{:S(2)}) collective-permute-start(bf16[3,8,2048]{2,1,0:T(8,128)(2,1)S(1)} %broadcast_select_fusion.1), channel_id=1, source_target_pairs={{0,112},{16,128},{32,176},{48,64},{64,48},{80,192},{96,240},{112,0... | collective-permute-start | bytes 294920 | tf_op jit(solution)/shard_map/ppermute | solution.py:261
  15.8 16.5 %collective-permute-start.8 = (bf16[3,8,4096]{2,1,0:T(8,128)(2,1)S(1)}, bf16[3,8,4096]{2,1,0:T(8,128)(2,1)S(1)}, u32[]{:S(2)}, u32[]{:S(2)}) collective-permute-start(bf16[3,8,4096]{2,1,0:T(8,128)(2,1)S(1)} %bitcast.7), channel_id=1, source_target_pairs={{0,1},{1,0},{2,3},{3,2},{4,5},{5,4},{6,7},{7,6},{8,9},{9,8},{10,11... | collective-permute-start | bytes 589832 | tf_op jit(solution)/shard_map/ppermute | solution.py:278
  17.2 15.2 %collective-permute-start.7 = (bf16[3,8,4096]{2,1,0:T(8,128)(2,1)S(1)}, bf16[3,8,4096]{2,1,0:T(8,128)(2,1)S(1)}, u32[]{:S(2)}, u32[]{:S(2)}) collective-permute-start(bf16[3,8,4096]{2,1,0:T(8,128)(2,1)S(1)} %bitcast.8), channel_id=1, source_target_pairs={{0,15},{1,2},{2,1},{3,4},{4,3},{5,6},{6,5},{7,8},{8,7},{9,10},{10,... | collective-permute-start | bytes 589832 | tf_op jit(solution)/shard_map/ppermute | solution.py:278
  24.0 3.4 %collective-permute-start.4 = (bf16[3,8,2048]{2,1,0:T(8,128)(2,1)S(1)}, bf16[3,8,2048]{2,1,0:T(8,128)(2,1)S(1)}, u32[]{:S(2)}, u32[]{:S(2)}) collective-permute-start(bf16[3,8,2048]{2,1,0:T(8,128)(2,1)S(1)} %broadcast_select_fusion.2.mine), channel_id=1, source_target_pairs={{0,16},{16,0},{32,48},{48,32},{64,80},{80,64},{96,112},{112,96},{1... | collective-permute-start | bytes 294920 | tf_op jit(solution)/shard_map/ppermute | solution.py:261
  25.7 6.7 %collective-permute-start.6 = (bf16[3,8,2048]{2,1,0:T(8,128)(2,1)S(1)}, bf16[3,8,2048]{2,1,0:T(8,128)(2,1)S(1)}, u32[]{:S(2)}, u32[]{:S(2)}) collective-permute-start(bf16[3,8,2048]{2,1,0:T(8,128)(2,1)S(1)} %broadcast_select_fusion.2.mine), channel_id=1, source_target_pairs={{0,1},{1,0},{2,3},{3,2},{4,5},{5,4},{6,7},{7,6},{8,9},{9,8},{10,11... | collective-permute-start | bytes 294920 | tf_op jit(solution)/shard_map/ppermute | solution.py:278
  25.7 7.8 %collective-permute-start.5 = (bf16[3,8,2048]{2,1,0:T(8,128)(2,1)S(1)}, bf16[3,8,2048]{2,1,0:T(8,128)(2,1)S(1)}, u32[]{:S(2)}, u32[]{:S(2)}) collective-permute-start(bf16[3,8,2048]{2,1,0:T(8,128)(2,1)S(1)} %broadcast_select_fusion.2.mine), channel_id=1, source_target_pairs={{0,15},{1,2},{2,1},{3,4},{4,3},{5,6},{6,5},{7,8},{8,7},{9,10},{10,... | collective-permute-start | bytes 294920 | tf_op jit(solution)/shard_map/ppermute | solution.py:278
  33.5 2.0 %collective-permute-start.9 = (bf16[3,8,2048]{2,1,0:T(8,128)(2,1)S(1)}, bf16[3,8,2048]{2,1,0:T(8,128)(2,1)S(1)}, u32[]{:S(2)}, u32[]{:S(2)}) collective-permute-start(bf16[3,8,2048]{2,1,0:T(8,128)(2,1)S(1)} %collective-permute-done.5.first_mine), channel_id=1, source_target_pairs={{0,16},{16,0},{32,48},{48,32},{64,80},{80,64},{96,112},{112,96},{1... | collective-permute-start | bytes 294920 | tf_op jit(solution)/shard_map/ppermute | solution.py:261
  34.5 1.3 %collective-permute-start.10 = (bf16[3,8,2048]{2,1,0:T(8,128)(2,1)S(1)}, bf16[3,8,2048]{2,1,0:T(8,128)(2,1)S(1)}, u32[]{:S(2)}, u32[]{:S(2)}) collective-permute-start(bf16[3,8,2048]{2,1,0:T(8,128)(2,1)S(1)} %collective-permute-done.6.second_mine), channel_id=1, source_target_pairs={{0,16},{16,0},{32,48},{48,32},{64,80},{80,64},{96,112},{112,96},{1... | collective-permute-start | bytes 294920 | tf_op jit(solution)/shard_map/ppermute | solution.py:261

commit v4 on v3

--- a/solution.py
+++ b/solution.py
@@ -289,7 +289,8 @@
     cut = lambda v: jnp.where(kind == 0, v[:, :, :half], v[:, :, half:])
     first, second = swap_slabs(x)
     from_mate = swap(x, "orb", lambda i: 1)
-    mine = jnp.where(me == owner, cut(x), cut(from_mate))
+    own_half = lax.optimization_barrier(cut(x))
+    mine = jnp.where(me == owner, own_half, cut(from_mate))
     known = 1
     for by_kind in ((8, 2), (2, 6), (6, 8)):
         theirs = swap(mine, "orb", lambda i: by_kind[kind_of(i)] ^ 1)

time: 52.7 us -> 52 us (0.987)
  transfers between devices with their start and end apart: 11 -> 11, of which waited for: 6 -> 5; matrix products, arithmetic and copies ran while one was open for 0% -> 2% of each run, Pallas kernels for 9% -> 9%
where the time goes in v4:
time: 52 us; the launch traced here: 51.8 us
  starting transfers between devices  17.1 us (33%)
  blocking collectives  12.4 us (24%)
  waiting for transfers between devices  10.8 us (21%)
  Pallas kernels  8.46 us (16%)
  other arithmetic  1.63 us (3%)
  between operations  1.39 us (3%)
    all_to_all x1, blocking collectives, on_device(): lax.all_to_all(jnp.broadcast_to(total[None], (lax.axis_size('dom'), OWN,...  12.4 us
    ppermute x4, starting transfers between devices, swap_one(): return lax.ppermute(x, axes, pairs)  9.72 us
    ppermute x7, waiting for transfers between devices, swap(): return lax.ppermute(x, axis, [(i, i ^ bits_of(i)) for i in range(size)])  9.67 us
    ppermute x7, starting transfers between devices, swap(): return lax.ppermute(x, axis, [(i, i ^ bits_of(i)) for i in range(size)])  7.4 us
    pallas_call x1, Pallas kernels, inner(): pl.pallas_call(inner_kernel, out_shape=jax.ShapeDtypeStruct(SUMS, jnp.flo...  4.89 us
    pallas_call x1, Pallas kernels, outer(): pl.pallas_call(outer_kernel, out_shape=(jax.ShapeDtypeStruct((DEPTH, OWN,...  3.57 us
    ppermute x4, waiting for transfers between devices, swap_one(): return lax.ppermute(x, axes, pairs)  1.16 us
  transfers between devices with their start and end apart: 11, of which 5 were waited for; matrix products, arithmetic and copies ran while one was open for 2% of the time, Pallas kernels for 9%

profile of v4, /device:TPU:1, one launch (start us, length us, event | category | flops | bytes accessed | tf_op | source)
XLA Modules:
  0.0 51.8 jit_solution(10085638610334371500)
XLA Ops:
  0.6 3.3 %collective-permute-start = (bf16[3,8,4096]{2,1,0:T(8,128)(2,1)}, bf16[3,8,4096]{2,1,0:T(8,128)(2,1)S(1)}, u32[]{:S(2)}, u32[]{:S(2)}) collective-permute-start(bf16[3,8,4096]{2,1,0:T(8,128)(2,1)} %bitcast.5), channel_id=1, source_target_pairs={{0,16},{16,0},{32,48},{48,32},{64,80},{80,64},{96,112},{112,96},{1... | collective-permute-start | bytes 589832 | tf_op jit(solution)/shard_map/ppermute | solution.py:261
  4.0 1.0 %slice_select_fusion.1 = bf16[3,8,2048]{2,1,0:T(8,128)(2,1)S(1)} fusion(bf16[3,8,4096]{2,1,0:T(8,128)(2,1)} %bitcast.6, pred[]{:T(512)S(6)} %eq.18), kind=kLoop, calls=%fused_computation.2 | loop fusion | flops 49152 | bytes 294913 | tf_op jit(solution)/shard_map/jit(_where)/select_n | solution.py:289
  5.6 0.0 collective-permute-done
  5.6 0.1 collective-permute-start.1
  5.7 4.0 %collective-permute-done.1 = bf16[3,8,2048]{2,1,0:T(8,128)(2,1)S(1)} collective-permute-done((bf16[3,8,2048]{2,1,0:T(8,128)(2,1)S(1)}, bf16[3,8,2048]{2,1,0:T(8,128)(2,1)S(1)}, u32[]{:S(2)}, u32[]{:S(2)}) %collective-permute-start.1) | collective-permute-done | bytes 98336 | tf_op jit(solution)/shard_map/ppermute | solution.py:261
  9.7 0.0 copy-start
  9.8 1.0 %collective-permute-start.2 = (bf16[3,8,2048]{2,1,0:T(8,128)(2,1)S(1)}, bf16[3,8,2048]{2,1,0:T(8,128)(2,1)S(1)}, u32[]{:S(2)}, u32[]{:S(2)}) collective-permute-start(bf16[3,8,2048]{2,1,0:T(8,128)(2,1)S(1)} %broadcast_select_fusion), channel_id=1, source_target_pairs={{0,48},{16,96},{32,80},{48,0},{64,112},{80,32},{96,16},{112,64},{1... | collective-permute-start | bytes 294920 | tf_op jit(solution)/shard_map/ppermute | solution.py:261
  10.8 4.3 %collective-permute-done.2 = bf16[3,8,2048]{2,1,0:T(8,128)(2,1)S(1)} collective-permute-done((bf16[3,8,2048]{2,1,0:T(8,128)(2,1)S(1)}, bf16[3,8,2048]{2,1,0:T(8,128)(2,1)S(1)}, u32[]{:S(2)}, u32[]{:S(2)}) %collective-permute-start.2) | collective-permute-done | bytes 98336 | tf_op jit(solution)/shard_map/ppermute | solution.py:261
  15.1 0.1 collective-permute-start.3
  15.2 0.0 copy-done
  15.2 1.2 %collective-permute-start.8 = (bf16[3,8,4096]{2,1,0:T(8,128)(2,1)S(1)}, bf16[3,8,4096]{2,1,0:T(8,128)(2,1)S(1)}, u32[]{:S(2)}, u32[]{:S(2)}) collective-permute-start(bf16[3,8,4096]{2,1,0:T(8,128)(2,1)S(1)} %bitcast.7), channel_id=1, source_target_pairs={{0,1},{1,0},{2,3},{3,2},{4,5},{5,4},{6,7},{7,6},{8,9},{9,8},{10,11... | collective-permute-start | bytes 589832 | tf_op jit(solution)/shard_map/ppermute | solution.py:278
  16.4 6.8 %collective-permute-start.7 = (bf16[3,8,4096]{2,1,0:T(8,128)(2,1)S(1)}, bf16[3,8,4096]{2,1,0:T(8,128)(2,1)S(1)}, u32[]{:S(2)}, u32[]{:S(2)}) collective-permute-start(bf16[3,8,4096]{2,1,0:T(8,128)(2,1)S(1)} %bitcast.8), channel_id=1, source_target_pairs={{0,15},{1,2},{2,1},{3,4},{4,3},{5,6},{6,5},{7,8},{8,7},{9,10},{10,... | collective-permute-start | bytes 589832 | tf_op jit(solution)/shard_map/ppermute | solution.py:278
  23.2 0.0 collective-permute-done.3
  23.2 1.9 %collective-permute-start.4 = (bf16[3,8,2048]{2,1,0:T(8,128)(2,1)S(1)}, bf16[3,8,2048]{2,1,0:T(8,128)(2,1)S(1)}, u32[]{:S(2)}, u32[]{:S(2)}) collective-permute-start(bf16[3,8,2048]{2,1,0:T(8,128)(2,1)S(1)} %broadcast_select_fusion.2.mine), channel_id=1, source_target_pairs={{0,16},{16,0},{32,48},{48,32},{64,80},{80,64},{96,112},{112,96},{1... | collective-permute-start | bytes 294920 | tf_op jit(solution)/shard_map/ppermute | solution.py:261
  25.1 0.0 collective-permute-start.6
  25.1 1.7 %collective-permute-start.5 = (bf16[3,8,2048]{2,1,0:T(8,128)(2,1)S(1)}, bf16[3,8,2048]{2,1,0:T(8,128)(2,1)S(1)}, u32[]{:S(2)}, u32[]{:S(2)}) collective-permute-start(bf16[3,8,2048]{2,1,0:T(8,128)(2,1)S(1)} %broadcast_select_fusion.2.mine), channel_id=1, source_target_pairs={{0,15},{1,2},{2,1},{3,4},{4,3},{5,6},{6,5},{7,8},{8,7},{9,10},{10,... | collective-permute-start | bytes 294920 | tf_op jit(solution)/shard_map/ppermute | solution.py:278
  26.9 0.0 collective-permute-done.4.other
  26.9 4.9 %shard_map.41.acc_in = f32[3,256,128]{2,1,0:T(8,128)S(1)} custom-call(bf16[3,8,2048]{2,1,0:T(8,128)(2,1)S(1)} %broadcast_select_fusion.2.mine, bf16[3,8,2048]{2,1,0:T(8,128)(2,1)S(1)} %collective-permute-done.4.other, bf16[3,8,4096]{2,1,0:T(8,128)(2,1)S(1)} %bitcast.9), custom_call_target="tpu_custom_call" | custom-call | flops 40000000 | bytes 1000000 | tf_op jit(solution)/shard_map/pallas_call | solution.py:227
  31.7 0.0 collective-permute-done.8.second
  31.8 0.0 collective-permute-done.7.first
  31.8 0.0 collective-permute-done.6.second_mine
  31.8 1.2 %collective-permute-done.5.first_mine = bf16[3,8,2048]{2,1,0:T(8,128)(2,1)S(1)} collective-permute-done((bf16[3,8,2048]{2,1,0:T(8,128)(2,1)S(1)}, bf16[3,8,2048]{2,1,0:T(8,128)(2,1)S(1)}, u32[]{:S(2)}, u32[]{:S(2)}) %collective-permute-start.5) | collective-permute-done | bytes 98336 | tf_op jit(solution)/shard_map/ppermute | solution.py:278
  32.9 1.0 %collective-permute-start.9 = (bf16[3,8,2048]{2,1,0:T(8,128)(2,1)S(1)}, bf16[3,8,2048]{2,1,0:T(8,128)(2,1)S(1)}, u32[]{:S(2)}, u32[]{:S(2)}) collective-permute-start(bf16[3,8,2048]{2,1,0:T(8,128)(2,1)S(1)} %collective-permute-done.5.first_mine), channel_id=1, source_target_pairs={{0,16},{16,0},{32,48},{48,32},{64,80},{80,64},{96,112},{112,96},{1... | collective-permute-start | bytes 294920 | tf_op jit(solution)/shard_map/ppermute | solution.py:261
  33.9 0.0 collective-permute-start.10
  33.9 0.9 %collective-permute-done.9.first_other = bf16[3,8,2048]{2,1,0:T(8,128)(2,1)S(1)} collective-permute-done((bf16[3,8,2048]{2,1,0:T(8,128)(2,1)S(1)}, bf16[3,8,2048]{2,1,0:T(8,128)(2,1)S(1)}, u32[]{:S(2)}, u32[]{:S(2)}) %collective-permute-start.9) | collective-permute-done | bytes 98336 | tf_op jit(solution)/shard_map/ppermute | solution.py:261
  34.9 0.4 collective-permute-done.10.second_other
  35.2 3.6 %shard_map.42 = (bf16[3,8,4096]{2,1,0:T(8,128)(2,1)}, f32[8,8]{1,0:T(8,128)S(1)}) custom-call(bf16[3,8,2048]{2,1,0:T(8,128)(2,1)S(1)} %broadcast_select_fusion.2.mine, bf16[3,8,2048]{2,1,0:T(8,128)(2,1)S(1)} %collective-permute-done.4.other, bf16[3,8,4096]{2,1,0:T(8,128)(2,1)S(1)} %collective-permute-done.7.first, ...), custom_call_target="tpu_custom_call" | custom-call | flops 20000000 | bytes 2000000 | tf_op jit(solution)/shard_map/pallas_call | solution.py:241
  38.8 12.4 %all_to_all.5 = f32[16,8,8]{2,1,0:T(8,128)S(1)} all-to-all(f32[16,8,8]{2,1,0:T(8,128)S(1)} %broadcast_in_dim.2), channel_id=1, replica_groups=mesh['orb'=16,'dom'=16] {'dom'}, dimensions={0} | all-to-all | bytes 8192 | tf_op jit(solution)/shard_map/all_to_all | solution.py:306
  51.2 0.6 %broadcast_multiply_fusion = f32[8,8]{1,0:T(8,128)} fusion(f32[8,8]{1,0:T(8,128)S(1)} %reduce_sum.9), kind=kLoop, calls=%fused_computation.6 | loop fusion | flops 64 | bytes 512 | tf_op jit(solution)/shard_map/div | solution.py:309
  (6 shorter events, 0.1 us)
Async XLA Ops:
  0.6 4.9 %collective-permute-start = (bf16[3,8,4096]{2,1,0:T(8,128)(2,1)}, bf16[3,8,4096]{2,1,0:T(8,128)(2,1)S(1)}, u32[]{:S(2)}, u32[]{:S(2)}) collective-permute-start(bf16[3,8,4096]{2,1,0:T(8,128)(2,1)} %bitcast.5), channel_id=1, source_target_pairs={{0,16},{16,0},{32,48},{48,32},{64,80},{80,64},{96,112},{112,96},{1... | collective-permute-start | bytes 589832 | tf_op jit(solution)/shard_map/ppermute | solution.py:261
  5.6 4.1 %collective-permute-start.1 = (bf16[3,8,2048]{2,1,0:T(8,128)(2,1)S(1)}, bf16[3,8,2048]{2,1,0:T(8,128)(2,1)S(1)}, u32[]{:S(2)}, u32[]{:S(2)}) collective-permute-start(bf16[3,8,2048]{2,1,0:T(8,128)(2,1)S(1)} %fusion), channel_id=1, source_target_pairs={{0,144},{16,32},{32,16},{48,160},{64,208},{80,96},{96,80},{112,224... | collective-permute-start | bytes 294920 | tf_op jit(solution)/shard_map/ppermute | solution.py:261
  9.7 5.5 %copy-start = (bf16[8,3,4096]{2,0,1:T(8,128)(2,1)S(1)}, bf16[8,3,4096]{2,0,1:T(8,128)(2,1)}, u32[]{:S(2)}) copy-start(bf16[8,3,4096]{2,0,1:T(8,128)(2,1)} %param.2) | copy-start | bytes 589828
  9.8 5.3 %collective-permute-start.2 = (bf16[3,8,2048]{2,1,0:T(8,128)(2,1)S(1)}, bf16[3,8,2048]{2,1,0:T(8,128)(2,1)S(1)}, u32[]{:S(2)}, u32[]{:S(2)}) collective-permute-start(bf16[3,8,2048]{2,1,0:T(8,128)(2,1)S(1)} %broadcast_select_fusion), channel_id=1, source_target_pairs={{0,48},{16,96},{32,80},{48,0},{64,112},{80,32},{96,16},{112,64},{1... | collective-permute-start | bytes 294920 | tf_op jit(solution)/shard_map/ppermute | solution.py:261
  15.1 8.1 %collective-permute-start.3 = (bf16[3,8,2048]{2,1,0:T(8,128)(2,1)S(1)}, bf16[3,8,2048]{2,1,0:T(8,128)(2,1)S(1)}, u32[]{:S(2)}, u32[]{:S(2)}) collective-permute-start(bf16[3,8,2048]{2,1,0:T(8,128)(2,1)S(1)} %broadcast_select_fusion.1), channel_id=1, source_target_pairs={{0,112},{16,128},{32,176},{48,64},{64,48},{80,192},{96,240},{112,0... | collective-permute-start | bytes 294920 | tf_op jit(solution)/shard_map/ppermute | solution.py:261
  15.2 16.5 %collective-permute-start.8 = (bf16[3,8,4096]{2,1,0:T(8,128)(2,1)S(1)}, bf16[3,8,4096]{2,1,0:T(8,128)(2,1)S(1)}, u32[]{:S(2)}, u32[]{:S(2)}) collective-permute-start(bf16[3,8,4096]{2,1,0:T(8,128)(2,1)S(1)} %bitcast.7), channel_id=1, source_target_pairs={{0,1},{1,0},{2,3},{3,2},{4,5},{5,4},{6,7},{7,6},{8,9},{9,8},{10,11... | collective-permute-start | bytes 589832 | tf_op jit(solution)/shard_map/ppermute | solution.py:278
  16.4 15.4 %collective-permute-start.7 = (bf16[3,8,4096]{2,1,0:T(8,128)(2,1)S(1)}, bf16[3,8,4096]{2,1,0:T(8,128)(2,1)S(1)}, u32[]{:S(2)}, u32[]{:S(2)}) collective-permute-start(bf16[3,8,4096]{2,1,0:T(8,128)(2,1)S(1)} %bitcast.8), channel_id=1, source_target_pairs={{0,15},{1,2},{2,1},{3,4},{4,3},{5,6},{6,5},{7,8},{8,7},{9,10},{10,... | collective-permute-start | bytes 589832 | tf_op jit(solution)/shard_map/ppermute | solution.py:278
  23.2 3.6 %collective-permute-start.4 = (bf16[3,8,2048]{2,1,0:T(8,128)(2,1)S(1)}, bf16[3,8,2048]{2,1,0:T(8,128)(2,1)S(1)}, u32[]{:S(2)}, u32[]{:S(2)}) collective-permute-start(bf16[3,8,2048]{2,1,0:T(8,128)(2,1)S(1)} %broadcast_select_fusion.2.mine), channel_id=1, source_target_pairs={{0,16},{16,0},{32,48},{48,32},{64,80},{80,64},{96,112},{112,96},{1... | collective-permute-start | bytes 294920 | tf_op jit(solution)/shard_map/ppermute | solution.py:261
  25.1 6.7 %collective-permute-start.6 = (bf16[3,8,2048]{2,1,0:T(8,128)(2,1)S(1)}, bf16[3,8,2048]{2,1,0:T(8,128)(2,1)S(1)}, u32[]{:S(2)}, u32[]{:S(2)}) collective-permute-start(bf16[3,8,2048]{2,1,0:T(8,128)(2,1)S(1)} %broadcast_select_fusion.2.mine), channel_id=1, source_target_pairs={{0,1},{1,0},{2,3},{3,2},{4,5},{5,4},{6,7},{7,6},{8,9},{9,8},{10,11... | collective-permute-start | bytes 294920 | tf_op jit(solution)/shard_map/ppermute | solution.py:278
  25.1 7.8 %collective-permute-start.5 = (bf16[3,8,2048]{2,1,0:T(8,128)(2,1)S(1)}, bf16[3,8,2048]{2,1,0:T(8,128)(2,1)S(1)}, u32[]{:S(2)}, u32[]{:S(2)}) collective-permute-start(bf16[3,8,2048]{2,1,0:T(8,128)(2,1)S(1)} %broadcast_select_fusion.2.mine), channel_id=1, source_target_pairs={{0,15},{1,2},{2,1},{3,4},{4,3},{5,6},{6,5},{7,8},{8,7},{9,10},{10,... | collective-permute-start | bytes 294920 | tf_op jit(solution)/shard_map/ppermute | solution.py:278
  32.9 2.0 %collective-permute-start.9 = (bf16[3,8,2048]{2,1,0:T(8,128)(2,1)S(1)}, bf16[3,8,2048]{2,1,0:T(8,128)(2,1)S(1)}, u32[]{:S(2)}, u32[]{:S(2)}) collective-permute-start(bf16[3,8,2048]{2,1,0:T(8,128)(2,1)S(1)} %collective-permute-done.5.first_mine), channel_id=1, source_target_pairs={{0,16},{16,0},{32,48},{48,32},{64,80},{80,64},{96,112},{112,96},{1... | collective-permute-start | bytes 294920 | tf_op jit(solution)/shard_map/ppermute | solution.py:261
  33.9 1.3 %collective-permute-start.10 = (bf16[3,8,2048]{2,1,0:T(8,128)(2,1)S(1)}, bf16[3,8,2048]{2,1,0:T(8,128)(2,1)S(1)}, u32[]{:S(2)}, u32[]{:S(2)}) collective-permute-start(bf16[3,8,2048]{2,1,0:T(8,128)(2,1)S(1)} %collective-permute-done.6.second_mine), channel_id=1, source_target_pairs={{0,16},{16,0},{32,48},{48,32},{64,80},{80,64},{96,112},{112,96},{1... | collective-permute-start | bytes 294920 | tf_op jit(solution)/shard_map/ppermute | solution.py:261

commit v5 on v4

--- a/solution.py
+++ b/solution.py
@@ -141,7 +141,7 @@
                 acc_out[z, pl.ds(tile * (8 * OWN) + j, 8, stride=OWN), :] = total[j]
         return carry
 
-    lax.fori_loop(0, ROWS // 8, tile_step, 0)
+    lax.fori_loop(0, ROWS // 8, tile_step, 0, unroll=acc_in is not None)
 
 
 INSIDE = [

time: 52 us -> 51.7 us (level)
  no operation moved by 1% of the time
where the time goes in v5:
time: 51.7 us; the launch traced here: 51.5 us
  starting transfers between devices  17.1 us (33%)
  blocking collectives  12.4 us (24%)
  waiting for transfers between devices  10.8 us (21%)
  Pallas kernels  8.15 us (16%)
  other arithmetic  1.63 us (3%)
  between operations  1.39 us (3%)
    all_to_all x1, blocking collectives, on_device(): lax.all_to_all(jnp.broadcast_to(total[None], (lax.axis_size('dom'), OWN,...  12.4 us
    ppermute x4, starting transfers between devices, swap_one(): return lax.ppermute(x, axes, pairs)  9.72 us
    ppermute x7, waiting for transfers between devices, swap(): return lax.ppermute(x, axis, [(i, i ^ bits_of(i)) for i in range(size)])  9.67 us
    ppermute x7, starting transfers between devices, swap(): return lax.ppermute(x, axis, [(i, i ^ bits_of(i)) for i in range(size)])  7.4 us
    pallas_call x1, Pallas kernels, inner(): pl.pallas_call(inner_kernel, out_shape=jax.ShapeDtypeStruct(SUMS, jnp.flo...  4.89 us
    pallas_call x1, Pallas kernels, outer(): pl.pallas_call(outer_kernel, out_shape=(jax.ShapeDtypeStruct((DEPTH, OWN,...  3.27 us
    ppermute x4, waiting for transfers between devices, swap_one(): return lax.ppermute(x, axes, pairs)  1.16 us
  transfers between devices with their start and end apart: 11, of which 5 were waited for; matrix products, arithmetic and copies ran while one was open for 2% of the time, Pallas kernels for 9%

profile of v5, /device:TPU:1, one launch (start us, length us, event | category | flops | bytes accessed | tf_op | source)
XLA Modules:
  0.0 51.5 jit_solution(6561290571906435846)
XLA Ops:
  0.6 3.3 %collective-permute-start = (bf16[3,8,4096]{2,1,0:T(8,128)(2,1)}, bf16[3,8,4096]{2,1,0:T(8,128)(2,1)S(1)}, u32[]{:S(2)}, u32[]{:S(2)}) collective-permute-start(bf16[3,8,4096]{2,1,0:T(8,128)(2,1)} %bitcast.5), channel_id=1, source_target_pairs={{0,16},{16,0},{32,48},{48,32},{64,80},{80,64},{96,112},{112,96},{1... | collective-permute-start | bytes 589832 | tf_op jit(solution)/shard_map/ppermute | solution.py:261
  4.0 1.0 %slice_select_fusion.1 = bf16[3,8,2048]{2,1,0:T(8,128)(2,1)S(1)} fusion(bf16[3,8,4096]{2,1,0:T(8,128)(2,1)} %bitcast.6, pred[]{:T(512)S(6)} %eq.18), kind=kLoop, calls=%fused_computation.2 | loop fusion | flops 49152 | bytes 294913 | tf_op jit(solution)/shard_map/jit(_where)/select_n | solution.py:289
  5.6 0.0 collective-permute-done
  5.6 0.1 collective-permute-start.1
  5.7 4.0 %collective-permute-done.1 = bf16[3,8,2048]{2,1,0:T(8,128)(2,1)S(1)} collective-permute-done((bf16[3,8,2048]{2,1,0:T(8,128)(2,1)S(1)}, bf16[3,8,2048]{2,1,0:T(8,128)(2,1)S(1)}, u32[]{:S(2)}, u32[]{:S(2)}) %collective-permute-start.1) | collective-permute-done | bytes 98336 | tf_op jit(solution)/shard_map/ppermute | solution.py:261
  9.7 0.0 copy-start
  9.8 1.0 %collective-permute-start.2 = (bf16[3,8,2048]{2,1,0:T(8,128)(2,1)S(1)}, bf16[3,8,2048]{2,1,0:T(8,128)(2,1)S(1)}, u32[]{:S(2)}, u32[]{:S(2)}) collective-permute-start(bf16[3,8,2048]{2,1,0:T(8,128)(2,1)S(1)} %broadcast_select_fusion), channel_id=1, source_target_pairs={{0,48},{16,96},{32,80},{48,0},{64,112},{80,32},{96,16},{112,64},{1... | collective-permute-start | bytes 294920 | tf_op jit(solution)/shard_map/ppermute | solution.py:261
  10.8 4.3 %collective-permute-done.2 = bf16[3,8,2048]{2,1,0:T(8,128)(2,1)S(1)} collective-permute-done((bf16[3,8,2048]{2,1,0:T(8,128)(2,1)S(1)}, bf16[3,8,2048]{2,1,0:T(8,128)(2,1)S(1)}, u32[]{:S(2)}, u32[]{:S(2)}) %collective-permute-start.2) | collective-permute-done | bytes 98336 | tf_op jit(solution)/shard_map/ppermute | solution.py:261
  15.1 0.1 collective-permute-start.3
  15.2 0.0 copy-done
  15.2 1.2 %collective-permute-start.8 = (bf16[3,8,4096]{2,1,0:T(8,128)(2,1)S(1)}, bf16[3,8,4096]{2,1,0:T(8,128)(2,1)S(1)}, u32[]{:S(2)}, u32[]{:S(2)}) collective-permute-start(bf16[3,8,4096]{2,1,0:T(8,128)(2,1)S(1)} %bitcast.7), channel_id=1, source_target_pairs={{0,1},{1,0},{2,3},{3,2},{4,5},{5,4},{6,7},{7,6},{8,9},{9,8},{10,11... | collective-permute-start | bytes 589832 | tf_op jit(solution)/shard_map/ppermute | solution.py:278
  16.4 6.8 %collective-permute-start.7 = (bf16[3,8,4096]{2,1,0:T(8,128)(2,1)S(1)}, bf16[3,8,4096]{2,1,0:T(8,128)(2,1)S(1)}, u32[]{:S(2)}, u32[]{:S(2)}) collective-permute-start(bf16[3,8,4096]{2,1,0:T(8,128)(2,1)S(1)} %bitcast.8), channel_id=1, source_target_pairs={{0,15},{1,2},{2,1},{3,4},{4,3},{5,6},{6,5},{7,8},{8,7},{9,10},{10,... | collective-permute-start | bytes 589832 | tf_op jit(solution)/shard_map/ppermute | solution.py:278
  23.2 0.0 collective-permute-done.3
  23.2 1.9 %collective-permute-start.4 = (bf16[3,8,2048]{2,1,0:T(8,128)(2,1)S(1)}, bf16[3,8,2048]{2,1,0:T(8,128)(2,1)S(1)}, u32[]{:S(2)}, u32[]{:S(2)}) collective-permute-start(bf16[3,8,2048]{2,1,0:T(8,128)(2,1)S(1)} %broadcast_select_fusion.2.mine), channel_id=1, source_target_pairs={{0,16},{16,0},{32,48},{48,32},{64,80},{80,64},{96,112},{112,96},{1... | collective-permute-start | bytes 294920 | tf_op jit(solution)/shard_map/ppermute | solution.py:261
  25.1 0.0 collective-permute-start.6
  25.1 1.7 %collective-permute-start.5 = (bf16[3,8,2048]{2,1,0:T(8,128)(2,1)S(1)}, bf16[3,8,2048]{2,1,0:T(8,128)(2,1)S(1)}, u32[]{:S(2)}, u32[]{:S(2)}) collective-permute-start(bf16[3,8,2048]{2,1,0:T(8,128)(2,1)S(1)} %broadcast_select_fusion.2.mine), channel_id=1, source_target_pairs={{0,15},{1,2},{2,1},{3,4},{4,3},{5,6},{6,5},{7,8},{8,7},{9,10},{10,... | collective-permute-start | bytes 294920 | tf_op jit(solution)/shard_map/ppermute | solution.py:278
  26.9 0.0 collective-permute-done.4.other
  26.9 4.9 %shard_map.41.acc_in = f32[3,256,128]{2,1,0:T(8,128)S(1)} custom-call(bf16[3,8,2048]{2,1,0:T(8,128)(2,1)S(1)} %broadcast_select_fusion.2.mine, bf16[3,8,2048]{2,1,0:T(8,128)(2,1)S(1)} %collective-permute-done.4.other, bf16[3,8,4096]{2,1,0:T(8,128)(2,1)S(1)} %bitcast.9), custom_call_target="tpu_custom_call" | custom-call | flops 40000000 | bytes 1000000 | tf_op jit(solution)/shard_map/pallas_call | solution.py:227
  31.7 0.0 collective-permute-done.8.second
  31.8 0.0 collective-permute-done.7.first
  31.8 0.0 collective-permute-done.6.second_mine
  31.8 1.2 %collective-permute-done.5.first_mine = bf16[3,8,2048]{2,1,0:T(8,128)(2,1)S(1)} collective-permute-done((bf16[3,8,2048]{2,1,0:T(8,128)(2,1)S(1)}, bf16[3,8,2048]{2,1,0:T(8,128)(2,1)S(1)}, u32[]{:S(2)}, u32[]{:S(2)}) %collective-permute-start.5) | collective-permute-done | bytes 98336 | tf_op jit(solution)/shard_map/ppermute | solution.py:278
  32.9 1.0 %collective-permute-start.9 = (bf16[3,8,2048]{2,1,0:T(8,128)(2,1)S(1)}, bf16[3,8,2048]{2,1,0:T(8,128)(2,1)S(1)}, u32[]{:S(2)}, u32[]{:S(2)}) collective-permute-start(bf16[3,8,2048]{2,1,0:T(8,128)(2,1)S(1)} %collective-permute-done.5.first_mine), channel_id=1, source_target_pairs={{0,16},{16,0},{32,48},{48,32},{64,80},{80,64},{96,112},{112,96},{1... | collective-permute-start | bytes 294920 | tf_op jit(solution)/shard_map/ppermute | solution.py:261
  33.9 0.0 collective-permute-start.10
  33.9 0.9 %collective-permute-done.9.first_other = bf16[3,8,2048]{2,1,0:T(8,128)(2,1)S(1)} collective-permute-done((bf16[3,8,2048]{2,1,0:T(8,128)(2,1)S(1)}, bf16[3,8,2048]{2,1,0:T(8,128)(2,1)S(1)}, u32[]{:S(2)}, u32[]{:S(2)}) %collective-permute-start.9) | collective-permute-done | bytes 98336 | tf_op jit(solution)/shard_map/ppermute | solution.py:261
  34.9 0.4 collective-permute-done.10.second_other
  35.2 3.3 %shard_map.42 = (bf16[3,8,4096]{2,1,0:T(8,128)(2,1)}, f32[8,8]{1,0:T(8,128)S(1)}) custom-call(bf16[3,8,2048]{2,1,0:T(8,128)(2,1)S(1)} %broadcast_select_fusion.2.mine, bf16[3,8,2048]{2,1,0:T(8,128)(2,1)S(1)} %collective-permute-done.4.other, bf16[3,8,4096]{2,1,0:T(8,128)(2,1)S(1)} %collective-permute-done.7.first, ...), custom_call_target="tpu_custom_call" | custom-call | flops 20000000 | bytes 2000000 | tf_op jit(solution)/shard_map/pallas_call | solution.py:241
  38.5 12.4 %all_to_all.5 = f32[16,8,8]{2,1,0:T(8,128)S(1)} all-to-all(f32[16,8,8]{2,1,0:T(8,128)S(1)} %broadcast_in_dim.2), channel_id=1, replica_groups=mesh['orb'=16,'dom'=16] {'dom'}, dimensions={0} | all-to-all | bytes 8192 | tf_op jit(solution)/shard_map/all_to_all | solution.py:306
  50.9 0.6 %broadcast_multiply_fusion = f32[8,8]{1,0:T(8,128)} fusion(f32[8,8]{1,0:T(8,128)S(1)} %reduce_sum.9), kind=kLoop, calls=%fused_computation.6 | loop fusion | flops 64 | bytes 512 | tf_op jit(solution)/shard_map/div | solution.py:309
  (6 shorter events, 0.1 us)
Async XLA Ops:
  0.6 4.9 %collective-permute-start = (bf16[3,8,4096]{2,1,0:T(8,128)(2,1)}, bf16[3,8,4096]{2,1,0:T(8,128)(2,1)S(1)}, u32[]{:S(2)}, u32[]{:S(2)}) collective-permute-start(bf16[3,8,4096]{2,1,0:T(8,128)(2,1)} %bitcast.5), channel_id=1, source_target_pairs={{0,16},{16,0},{32,48},{48,32},{64,80},{80,64},{96,112},{112,96},{1... | collective-permute-start | bytes 589832 | tf_op jit(solution)/shard_map/ppermute | solution.py:261
  5.6 4.1 %collective-permute-start.1 = (bf16[3,8,2048]{2,1,0:T(8,128)(2,1)S(1)}, bf16[3,8,2048]{2,1,0:T(8,128)(2,1)S(1)}, u32[]{:S(2)}, u32[]{:S(2)}) collective-permute-start(bf16[3,8,2048]{2,1,0:T(8,128)(2,1)S(1)} %fusion), channel_id=1, source_target_pairs={{0,144},{16,32},{32,16},{48,160},{64,208},{80,96},{96,80},{112,224... | collective-permute-start | bytes 294920 | tf_op jit(solution)/shard_map/ppermute | solution.py:261
  9.7 5.5 %copy-start = (bf16[8,3,4096]{2,0,1:T(8,128)(2,1)S(1)}, bf16[8,3,4096]{2,0,1:T(8,128)(2,1)}, u32[]{:S(2)}) copy-start(bf16[8,3,4096]{2,0,1:T(8,128)(2,1)} %param.2) | copy-start | bytes 589828
  9.8 5.3 %collective-permute-start.2 = (bf16[3,8,2048]{2,1,0:T(8,128)(2,1)S(1)}, bf16[3,8,2048]{2,1,0:T(8,128)(2,1)S(1)}, u32[]{:S(2)}, u32[]{:S(2)}) collective-permute-start(bf16[3,8,2048]{2,1,0:T(8,128)(2,1)S(1)} %broadcast_select_fusion), channel_id=1, source_target_pairs={{0,48},{16,96},{32,80},{48,0},{64,112},{80,32},{96,16},{112,64},{1... | collective-permute-start | bytes 294920 | tf_op jit(solution)/shard_map/ppermute | solution.py:261
  15.1 8.1 %collective-permute-start.3 = (bf16[3,8,2048]{2,1,0:T(8,128)(2,1)S(1)}, bf16[3,8,2048]{2,1,0:T(8,128)(2,1)S(1)}, u32[]{:S(2)}, u32[]{:S(2)}) collective-permute-start(bf16[3,8,2048]{2,1,0:T(8,128)(2,1)S(1)} %broadcast_select_fusion.1), channel_id=1, source_target_pairs={{0,112},{16,128},{32,176},{48,64},{64,48},{80,192},{96,240},{112,0... | collective-permute-start | bytes 294920 | tf_op jit(solution)/shard_map/ppermute | solution.py:261
  15.2 16.5 %collective-permute-start.8 = (bf16[3,8,4096]{2,1,0:T(8,128)(2,1)S(1)}, bf16[3,8,4096]{2,1,0:T(8,128)(2,1)S(1)}, u32[]{:S(2)}, u32[]{:S(2)}) collective-permute-start(bf16[3,8,4096]{2,1,0:T(8,128)(2,1)S(1)} %bitcast.7), channel_id=1, source_target_pairs={{0,1},{1,0},{2,3},{3,2},{4,5},{5,4},{6,7},{7,6},{8,9},{9,8},{10,11... | collective-permute-start | bytes 589832 | tf_op jit(solution)/shard_map/ppermute | solution.py:278
  16.4 15.4 %collective-permute-start.7 = (bf16[3,8,4096]{2,1,0:T(8,128)(2,1)S(1)}, bf16[3,8,4096]{2,1,0:T(8,128)(2,1)S(1)}, u32[]{:S(2)}, u32[]{:S(2)}) collective-permute-start(bf16[3,8,4096]{2,1,0:T(8,128)(2,1)S(1)} %bitcast.8), channel_id=1, source_target_pairs={{0,15},{1,2},{2,1},{3,4},{4,3},{5,6},{6,5},{7,8},{8,7},{9,10},{10,... | collective-permute-start | bytes 589832 | tf_op jit(solution)/shard_map/ppermute | solution.py:278
  23.2 3.6 %collective-permute-start.4 = (bf16[3,8,2048]{2,1,0:T(8,128)(2,1)S(1)}, bf16[3,8,2048]{2,1,0:T(8,128)(2,1)S(1)}, u32[]{:S(2)}, u32[]{:S(2)}) collective-permute-start(bf16[3,8,2048]{2,1,0:T(8,128)(2,1)S(1)} %broadcast_select_fusion.2.mine), channel_id=1, source_target_pairs={{0,16},{16,0},{32,48},{48,32},{64,80},{80,64},{96,112},{112,96},{1... | collective-permute-start | bytes 294920 | tf_op jit(solution)/shard_map/ppermute | solution.py:261
  25.1 6.7 %collective-permute-start.6 = (bf16[3,8,2048]{2,1,0:T(8,128)(2,1)S(1)}, bf16[3,8,2048]{2,1,0:T(8,128)(2,1)S(1)}, u32[]{:S(2)}, u32[]{:S(2)}) collective-permute-start(bf16[3,8,2048]{2,1,0:T(8,128)(2,1)S(1)} %broadcast_select_fusion.2.mine), channel_id=1, source_target_pairs={{0,1},{1,0},{2,3},{3,2},{4,5},{5,4},{6,7},{7,6},{8,9},{9,8},{10,11... | collective-permute-start | bytes 294920 | tf_op jit(solution)/shard_map/ppermute | solution.py:278
  25.1 7.8 %collective-permute-start.5 = (bf16[3,8,2048]{2,1,0:T(8,128)(2,1)S(1)}, bf16[3,8,2048]{2,1,0:T(8,128)(2,1)S(1)}, u32[]{:S(2)}, u32[]{:S(2)}) collective-permute-start(bf16[3,8,2048]{2,1,0:T(8,128)(2,1)S(1)} %broadcast_select_fusion.2.mine), channel_id=1, source_target_pairs={{0,15},{1,2},{2,1},{3,4},{4,3},{5,6},{6,5},{7,8},{8,7},{9,10},{10,... | collective-permute-start | bytes 294920 | tf_op jit(solution)/shard_map/ppermute | solution.py:278
  32.9 2.0 %collective-permute-start.9 = (bf16[3,8,2048]{2,1,0:T(8,128)(2,1)S(1)}, bf16[3,8,2048]{2,1,0:T(8,128)(2,1)S(1)}, u32[]{:S(2)}, u32[]{:S(2)}) collective-permute-start(bf16[3,8,2048]{2,1,0:T(8,128)(2,1)S(1)} %collective-permute-done.5.first_mine), channel_id=1, source_target_pairs={{0,16},{16,0},{32,48},{48,32},{64,80},{80,64},{96,112},{112,96},{1... | collective-permute-start | bytes 294920 | tf_op jit(solution)/shard_map/ppermute | solution.py:261
  33.9 1.3 %collective-permute-start.10 = (bf16[3,8,2048]{2,1,0:T(8,128)(2,1)S(1)}, bf16[3,8,2048]{2,1,0:T(8,128)(2,1)S(1)}, u32[]{:S(2)}, u32[]{:S(2)}) collective-permute-start(bf16[3,8,2048]{2,1,0:T(8,128)(2,1)S(1)} %collective-permute-done.6.second_mine), channel_id=1, source_target_pairs={{0,16},{16,0},{32,48},{48,32},{64,80},{80,64},{96,112},{112,96},{1... | collective-permute-start | bytes 294920 | tf_op jit(solution)/shard_map/ppermute | solution.py:261
